TPU v7x, 32 devices: a whole 2x2x4 slice. The times are simulated.
32 devices in a mesh: circ: 8 (over z, x), axial: 4 (over y, core).
Axes of the slice: x: 2, y: 2, z: 4, core: 2. Of those that a mesh axis runs over, the one named last changes fastest.
Arguments:
- seal_state: float32 [12, 512, 512], P(None, 'circ', 'axial'), may hold values from -6 to 6
- seal_blocks: bfloat16 [5, 36, 512, 512], P(None, None, 'circ', 'axial'), may hold values from -0.875 to 0.875
- seal_scales: float32 [5, 512, 512], P(None, 'circ', 'axial'), may hold values from 0.3 to 3
- seal_volume: float32 [512, 512], P('circ', 'axial'), may hold values from 0.3 to 3
- cavity_state: float32 [12, 32768], P(None, ('circ', 'axial')), may hold values from -6 to 6
- cavity_blocks: bfloat16 [5, 36, 32768], P(None, None, ('circ', 'axial')), may hold values from -0.875 to 0.875
- cavity_scales: float32 [5, 32768], P(None, ('circ', 'axial')), may hold values from 0.3 to 3
- cavity_links: int32 [4, 32768], P(None, ('circ', 'axial')), may hold values from 0 to 1023
- cavity_volume: float32 [32768], P(('circ', 'axial')), may hold values from 0.3 to 3
- link_owner: int32 [65536, 1], P(('circ', 'axial')), may hold values from 0 to 7; in each aligned block of 2048 rows (0 to 2047, 2048 to 4095, ...) at most 512 rows name the same one
- link_seal: int32 [65536], P(('circ', 'axial')), may hold values from 0 to 8191
- link_cavity: int32 [65536], P(('circ', 'axial')), may hold values from 0 to 1023
- link_blocks: bfloat16 [2, 36, 65536], P(None, None, ('circ', 'axial')), may hold values from -0.875 to 0.875
- link_scales: float32 [2, 65536], P(None, ('circ', 'axial')), may hold values from 0.3 to 3
Outputs:
- seal_residual: float32 [12, 512, 512], P(None, 'circ', 'axial')
- cavity_residual: float32 [12, 32768], P(None, ('circ', 'axial'))
Inputs may be any that keep to these rules, and one draw needn't show every extreme that they name: `link_owner`: among the rows of one device, no sector is named by more than 512 rows, and in every draw some device names some sector exactly 512 times.
All inputs are finite; a program needn't handle non-finite values.
Results may differ from a plain program's by a relative error of at most 0.0003.
Values may be sent and summed in bfloat16 or wider, within the bound.
No kernel may reach another device: no remote copies, remote signals or barrier semaphores. Data moves between devices by JAX's collectives and lax.ppermute only.
A program may use at most 64 MiB of HBM per device.

v0:
```python
import functools
import jax
import jax.numpy as jnp
from jax import lax
from jax.experimental import pallas as pl
from jax.experimental.pallas import tpu as pltpu
from jax.sharding import PartitionSpec as P

whirl_rate = 0.6
F32, BF16, I32 = jnp.float32, jnp.bfloat16, jnp.int32
LANES = 128
WIDE = 256
PARAMS = pltpu.CompilerParams(vmem_limit_bytes=40 * 1024 * 1024)
VMEM = pl.BlockSpec(memory_space=pltpu.VMEM)


def iota(shape, axis):
    return lax.broadcasted_iota(I32, shape, axis)


def lane_take(row, index):
    table = jnp.broadcast_to(row, index.shape)
    return jnp.take_along_axis(table, index, axis=1, mode="promise_in_bounds")


def halves(value):
    high = value.astype(BF16).astype(F32)
    return high, value - high


def product_into(totals, entry, factor, vector):
    for row in range(6):
        real_part = imag_part = None
        for col in range(6):
            element = entry(6 * row + col)
            real_term, imag_term = element * vector[col], element * vector[6 + col]
            real_part = real_term if real_part is None else real_part + real_term
            imag_part = imag_term if imag_part is None else imag_part + imag_term
        real_part, imag_part = factor * real_part, factor * imag_part
        totals[row] = real_part if totals[row] is None else totals[row] + real_part
        totals[6 + row] = imag_part if totals[6 + row] is None else totals[6 + row] + imag_part
    return totals


def whirl(vector, volume):
    weight = whirl_rate * volume
    return [-weight * v for v in vector[6:]] + [weight * v for v in vector[:6]]


def fold_cells(source, target, count, base, cells):
    rows = cells // LANES
    for chunk in range(rows):
        target[pl.ds(base + chunk, count, stride=rows), :] = source[:, chunk * LANES : (chunk + 1) * LANES]


def interface_kernel(
    sectors, halo_rows, owner, seal_index, cavity_index, state, blocks, scales, first, last,
    send, slots, block_rows, scale_rows, state_rows, left, right,
):
    rows = owner.shape[0]
    capacity = 2 * rows * LANES // sectors
    sector_id = iota((sectors, LANES), 0)
    hot = [
        jnp.where(sector_id == owner[c : c + 1, :], 1.0, 0.0).astype(F32) for c in range(rows)
    ]
    stacked = jnp.concatenate(hot, axis=0).astype(BF16)
    before = (iota((LANES, LANES), 0) < iota((LANES, LANES), 1)).astype(F32).astype(BF16)
    prefix = jnp.dot(stacked, before, preferred_element_type=F32)
    totals = jnp.dot(stacked, jnp.ones((LANES, LANES), BF16), preferred_element_type=F32)
    offset = jnp.zeros((sectors, LANES), F32)
    for c in range(rows):
        part = slice(c * sectors, (c + 1) * sectors)
        place = jnp.sum(hot[c] * (prefix[part] + offset), axis=0, keepdims=True)
        slots[c : c + 1, :] = owner[c : c + 1, :] * capacity + place.astype(I32)
        offset = offset + totals[part]
    for entry in range(36):
        both = blocks[entry].astype(F32)
        for c in range(rows):
            block_rows[pl.ds(entry * rows + c, 2, stride=36 * rows), :] = both[
                :, c * LANES : (c + 1) * LANES
            ]
    fold_cells(scales, scale_rows, 2, 0, rows * LANES)
    fold_cells(state, state_rows, 12, 0, state.shape[1])
    tile_rows = state.shape[1] // LANES
    cell = cavity_index[...]
    lane, high = cell & (LANES - 1), cell >> 7
    vector = [jnp.zeros((rows, LANES), F32)] * 12
    for r in range(tile_rows):
        here = high == r
        for f in range(12):
            row = state_rows[f * tile_rows + r : f * tile_rows + r + 1, :]
            vector[f] = jnp.where(here, lane_take(row, lane), vector[f])
    terms = product_into(
        [None] * 12, lambda e: block_rows[e * rows : (e + 1) * rows, :], scale_rows[0:rows, :], vector
    )
    terms.append(seal_index[...].astype(F32))
    parts = [half for term in terms for half in halves(term)]
    groups = 2 * rows * LANES // WIDE
    for c in range(rows):
        slot = slots[c : c + 1, :]
        cols = slice(c * LANES, (c + 1) * LANES)
        right[:, cols] = jnp.where(
            iota((WIDE, LANES), 0) == (slot & (WIDE - 1)), 1.0, 0.0
        ).astype(BF16)
        here = iota((groups, LANES), 0) == (slot >> 8)
        for number, part in enumerate(parts):
            left[number * groups : (number + 1) * groups, cols] = jnp.where(
                here, part[c : c + 1, :], 0.0
            ).astype(BF16)
    moved = lax.dot_general(
        left[...], right[...], (((1,), (1,)), ((), ())), preferred_element_type=F32
    )
    for number in range(13):
        pair = moved[2 * number * groups : (2 * number + 2) * groups]
        value = pair[:groups] + pair[groups:]
        for half in range(2):
            send[pl.ds(half * 16 + number, groups, stride=32), :] = value[
                :, half * LANES : (half + 1) * LANES
            ]
    for number in range(13, 16):
        send[pl.ds(number, 2 * groups, stride=16), :] = jnp.zeros((2 * groups, LANES), F32)
    if halo_rows:
        me = lax.axis_index("circ")
        for step, edge, row in ((1, last, 7), (sectors - 1, first, 0)):
            base = lax.rem(me + step, sectors) * 64
            for f in range(12):
                send[pl.ds(base + (f // 3) * 16 + 13 + f % 3, 1), :] = edge[f, row : row + 1, :]


def face_kernel(state, faces):
    lane = iota(faces.shape, 1)
    total = jnp.zeros(faces.shape, F32)
    for f in range(12):
        total = jnp.where(lane == f, pltpu.roll(state[f], f + 1, 1), total)
        total = jnp.where(lane == 16 + f, pltpu.roll(state[f], 16 + f, 1), total)
    faces[...] = total


def seal_kernel(step_rows, state, blocks, scales, volume, from_low, from_high, out, beside, along):
    rows = state.shape[1]

    @pl.when(pl.program_id(0) == 0)
    def _():
        lane = iota((rows, LANES), 1)
        low, high = from_low[...], from_high[...]
        for f in range(12):
            beside[0, f, 1:rows, :] = state[f, 0 : rows - 1, :]
            beside[0, f, 0:1, :] = jnp.zeros((1, LANES), F32)
            beside[1, f, 0 : rows - 1, :] = state[f, 1:rows, :]
            beside[1, f, rows - 1 : rows, :] = jnp.zeros((1, LANES), F32)
            own = state[f]
            edge = pltpu.roll(low, (LANES - f) % LANES, 1)
            along[0, f] = jnp.where(lane == 0, edge, pltpu.roll(own, 1, 1))
            edge = pltpu.roll(high, LANES - 1 - 16 - f, 1)
            along[1, f] = jnp.where(lane == LANES - 1, edge, pltpu.roll(own, LANES - 1, 1))

    start = pl.multiple_of(pl.program_id(0) * step_rows, step_rows)
    here = pl.ds(start, step_rows)
    own = [state[f, here, :] for f in range(12)]
    totals = whirl(own, volume[here, :])
    for number in range(5):
        if number == 0:
            vector = own
        else:
            source = beside if number < 3 else along
            vector = [source[(number - 1) % 2, f, here, :] for f in range(12)]
        totals = product_into(
            totals, lambda e: blocks[number, e].astype(F32), scales[number, here, :], vector
        )
    for f in range(12):
        out[f] = totals[f]


def answer_kernel(state, arrived, send):
    chunks = arrived.shape[0] // 16
    cell = arrived[pl.ds(12, chunks, stride=16), :].astype(I32)
    lane, high = cell & (LANES - 1), cell >> 7
    value = [jnp.zeros(cell.shape, F32)] * 12
    for r in range(state.shape[1]):
        here = high == r
        for f in range(12):
            value[f] = jnp.where(here, lane_take(state[f, r : r + 1, :], lane), value[f])
    for f in range(12):
        send[pl.ds(f, chunks, stride=12), :] = value[f]


def seal_add_kernel(
    halo_rows, sectors, part, arrived, blocks_low, blocks_high, scales, halo_low, halo_high,
    out, left, right, total,
):
    chunks = arrived.shape[0] // 16
    rows = part.shape[1]
    half_rows = rows // 2
    total[...] = jnp.zeros_like(total)
    deep = left.shape[1] // LANES

    def add_chunks(step, carry):
        for sub in range(deep):
            tile = arrived[pl.ds(pl.multiple_of((step * deep + sub) * 16, 16), 16), :]
            high, low = halves(tile)
            cell = tile[12:13, :].astype(I32)
            row = cell >> 7
            column = (cell & (LANES - 1)) + jnp.where(row >= half_rows, LANES, 0)
            row = jnp.where(row >= half_rows, row - half_rows, row)
            cols = slice(sub * LANES, (sub + 1) * LANES)
            right[:, cols] = jnp.where(iota((WIDE, LANES), 0) == column, 1.0, 0.0).astype(BF16)
            here = iota((half_rows, LANES), 0) == row
            for f in range(12):
                for number, source in enumerate((high, low)):
                    at = (2 * f + number) * half_rows
                    left[at : at + half_rows, cols] = jnp.where(
                        here, source[f : f + 1, :], 0.0
                    ).astype(BF16)
        total[...] += lax.dot_general(
            left[...], right[...], (((1,), (1,)), ((), ())), preferred_element_type=F32
        )
        return carry

    lax.fori_loop(0, chunks // deep, add_chunks, 0)
    for f in range(12):
        added = (
            total[2 * f * half_rows : (2 * f + 1) * half_rows, :]
            + total[(2 * f + 1) * half_rows : (2 * f + 2) * half_rows, :]
        )
        out[f, 0:half_rows, :] = part[f, 0:half_rows, :] + added[:, :LANES]
        out[f, half_rows:rows, :] = part[f, half_rows:rows, :] + added[:, LANES:]
    me = lax.axis_index("circ")
    edge = blocks_low.shape[2]
    for number, step, halo, blocks in ((1, sectors - 1, halo_low, blocks_low), (2, 1, halo_high, blocks_high)):
        if halo_rows:
            base = lax.rem(me + step, sectors) * 64
            vector = [
                arrived[pl.ds(base + (f // 3) * 16 + 13 + f % 3, 1), :] for f in range(12)
            ]
        else:
            vector = [halo[f] for f in range(12)]
        at = 0 if number == 1 else rows - 1
        inner = 0 if number == 1 else edge - 1
        terms = product_into(
            [None] * 12,
            lambda e: blocks[0, e].astype(F32)[inner : inner + 1, :],
            scales[number, at : at + 1, :],
            vector,
        )
        for f in range(12):
            out[f, at : at + 1, :] = out[f, at : at + 1, :] + terms[f]


def cavity_kernel(
    state, blocks, scales, links, volume, link_blocks,
    out, link_rows, state_rows, block_rows, scale_rows, face_rows, out_rows,
):
    cells = state.shape[1]
    rows = cells // LANES
    fold_cells(state, state_rows, 12, 0, cells)
    fold_cells(scales, scale_rows, 5, 0, cells)
    fold_cells(links, face_rows, 4, 0, cells)
    for number in range(5):
        for c in range(rows):
            block_rows[pl.ds(number * 36 * rows + c, 36, stride=rows), :] = blocks[
                number, :, c * LANES : (c + 1) * LANES
            ].astype(F32)
    own = [state_rows[f * rows : (f + 1) * rows, :] for f in range(12)]
    totals = whirl(own, volume[...])
    for number in range(5):
        if number == 0:
            vector = own
        else:
            cell = face_rows[(number - 1) * rows : number * rows, :]
            lane, high = cell & (LANES - 1), cell >> 7
            vector = [jnp.zeros((rows, LANES), F32)] * 12
            for r in range(rows):
                here = high == r
                for f in range(12):
                    row = state_rows[f * rows + r : f * rows + r + 1, :]
                    vector[f] = jnp.where(here, lane_take(row, lane), vector[f])
        base = number * 36 * rows
        totals = product_into(
            totals,
            lambda e: block_rows[base + e * rows : base + (e + 1) * rows, :],
            scale_rows[number * rows : (number + 1) * rows, :],
            vector,
        )
    for f in range(12):
        out_rows[f * rows : (f + 1) * rows, :] = totals[f]
    for c in range(rows):
        out[:, c * LANES : (c + 1) * LANES] = out_rows[pl.ds(c, 12, stride=rows), :]
    row_count = link_blocks.shape[2] // LANES
    for entry in range(36):
        both = link_blocks[entry].astype(F32)
        for c in range(row_count):
            link_rows[entry * row_count + c : entry * row_count + c + 1, :] = both[
                1:2, c * LANES : (c + 1) * LANES
            ]


def cavity_add_kernel(
    part, arrived, slots, cavity_index, link_rows, scales, out, scale_rows, left, right
):
    rows = slots.shape[0]
    chunks = arrived.shape[0] // 12
    slot = slots[...]
    lane, high = slot & (LANES - 1), slot >> 7
    vector = [jnp.zeros(slot.shape, F32)] * 12
    for chunk in range(chunks):
        here = high == chunk
        for f in range(12):
            row = arrived[chunk * 12 + f : chunk * 12 + f + 1, :]
            vector[f] = jnp.where(here, lane_take(row, lane), vector[f])
    fold_cells(scales, scale_rows, 2, 0, rows * LANES)
    terms = product_into(
        [None] * 12,
        lambda e: link_rows[e * rows : (e + 1) * rows, :],
        scale_rows[rows : 2 * rows, :],
        vector,
    )
    parts = [halves(term) for term in terms]
    bands = part.shape[1] // WIDE
    for c in range(rows):
        cell = cavity_index[c : c + 1, :]
        cols = slice(c * LANES, (c + 1) * LANES)
        right[:, cols] = jnp.where(iota((WIDE, LANES), 0) == (cell & (WIDE - 1)), 1.0, 0.0).astype(BF16)
        band = cell >> 8
        zero = jnp.zeros((4, LANES), F32)
        tile = jnp.concatenate(
            [p[0][c : c + 1, :] for p in parts] + [zero] + [p[1][c : c + 1, :] for p in parts] + [zero],
            axis=0,
        )
        for b in range(bands):
            left[b * 32 : (b + 1) * 32, cols] = jnp.where(band == b, tile, 0.0).astype(BF16)
    added = lax.dot_general(
        left[...], right[...], (((1,), (1,)), ((), ())), preferred_element_type=F32
    )
    for b in range(bands):
        cols = slice(b * WIDE, (b + 1) * WIDE)
        out[:, cols] = part[:, cols] + (added[b * 32 : b * 32 + 12] + added[b * 32 + 16 : b * 32 + 28])


def exchange(values, sectors, features):
    chunks = values.shape[0] // features
    if sectors <= chunks:
        shaped = values.reshape(sectors, chunks // sectors * features, LANES)
        moved = lax.all_to_all(shaped, "circ", split_axis=0, concat_axis=0, tiled=True)
        return moved.reshape(values.shape)
    each = sectors // chunks
    shaped = values.reshape(chunks, features, each, LANES // each).transpose(0, 2, 1, 3)
    shaped = shaped.reshape(sectors, features, LANES // each)
    moved = lax.all_to_all(shaped, "circ", split_axis=0, concat_axis=0, tiled=True)
    moved = moved.reshape(chunks, each, features, LANES // each).transpose(0, 2, 1, 3)
    return moved.reshape(values.shape)


def on_device(
    seal_state,
    seal_blocks,
    seal_scales,
    seal_volume,
    cavity_state,
    cavity_blocks,
    cavity_scales,
    cavity_links,
    cavity_volume,
    link_owner,
    link_seal,
    link_cavity,
    link_blocks,
    link_scales,
):
    sectors = lax.axis_size("circ")
    segments = lax.axis_size("axial")
    _, seal_rows, _ = seal_state.shape
    cells = cavity_state.shape[1]
    count = link_seal.shape[0]
    rows = count // LANES
    groups = 2 * count // WIDE
    halo_rows = sectors * 2 == groups
    shape = jax.ShapeDtypeStruct
    owner = link_owner.reshape(rows, LANES)
    seal_index = link_seal.reshape(rows, LANES)
    cavity_index = link_cavity.reshape(rows, LANES)
    pair_blocks = link_blocks.transpose(1, 0, 2)

    edge = lambda at: pl.BlockSpec((12, 8, LANES), lambda i: (0, at, 0))
    whole = lambda a: pl.BlockSpec(a.shape, lambda i: (0,) * len(a.shape))
    head = (owner, seal_index, cavity_index, cavity_state, pair_blocks, link_scales)
    send, slots = pl.pallas_call(
        functools.partial(interface_kernel, sectors, halo_rows),
        grid=(1,),
        in_specs=[whole(a) for a in head] + [edge(0), edge(seal_rows // 8 - 1)],
        out_specs=[
            pl.BlockSpec((groups * 32, LANES), lambda i: (0, 0)),
            pl.BlockSpec((rows, LANES), lambda i: (0, 0)),
        ],
        out_shape=[shape((groups * 32, LANES), F32), shape((rows, LANES), I32)],
        scratch_shapes=[
            pltpu.VMEM((72 * rows, LANES), F32),
            pltpu.VMEM((2 * rows, LANES), F32),
            pltpu.VMEM((12 * cells // LANES, LANES), F32),
            pltpu.VMEM((26 * groups, count), BF16),
            pltpu.VMEM((WIDE, count), BF16),
        ],
        compiler_params=PARAMS,
        name="interface",
    )(*head, seal_state, seal_state)
    arrived = exchange(send, sectors, 16)

    faces = pl.pallas_call(
        face_kernel,
        in_specs=[VMEM],
        out_specs=VMEM,
        out_shape=shape((seal_rows, LANES), F32),
        compiler_params=PARAMS,
        name="faces",
    )(seal_state)
    from_low = lax.ppermute(faces, "axial", [(i, i + 1) for i in range(segments - 1)])
    from_high = lax.ppermute(faces, "axial", [(i + 1, i) for i in range(segments - 1)])
    if halo_rows:
        halos = ()
    else:
        first, last = seal_state[:, :1], seal_state[:, -1:]
        halos = (
            lax.ppermute(last, "circ", [(i, (i + 1) % sectors) for i in range(sectors)]),
            lax.ppermute(first, "circ", [((i + 1) % sectors, i) for i in range(sectors)]),
        )

    cavity_part, link_rows = pl.pallas_call(
        cavity_kernel,
        in_specs=[VMEM] * 6,
        out_specs=[VMEM, VMEM],
        out_shape=[shape((12, cells), F32), shape((36 * rows, LANES), F32)],
        scratch_shapes=[
            pltpu.VMEM((12 * cells // LANES, LANES), F32),
            pltpu.VMEM((180 * cells // LANES, LANES), F32),
            pltpu.VMEM((5 * cells // LANES, LANES), F32),
            pltpu.VMEM((4 * cells // LANES, LANES), I32),
            pltpu.VMEM((12 * cells // LANES, LANES), F32),
        ],
        compiler_params=PARAMS,
        cost_estimate=pl.CostEstimate(flops=10**6, bytes_accessed=10**7, transcendentals=0),
        name="cavity",
    )(cavity_state, cavity_blocks, cavity_scales, cavity_links, cavity_volume.reshape(-1, LANES), pair_blocks)

    step_rows = 16
    seal_part = pl.pallas_call(
        functools.partial(seal_kernel, step_rows),
        grid=(seal_rows // step_rows,),
        in_specs=[
            whole(seal_state),
            pl.BlockSpec((5, 36, step_rows, LANES), lambda i: (0, 0, i, 0)),
            whole(seal_scales),
            whole(seal_volume),
            whole(faces),
            whole(faces),
        ],
        out_specs=pl.BlockSpec((12, step_rows, LANES), lambda i: (0, i, 0)),
        out_shape=shape(seal_state.shape, F32),
        scratch_shapes=[
            pltpu.VMEM((2,) + seal_state.shape, F32),
            pltpu.VMEM((2,) + seal_state.shape, F32),
        ],
        compiler_params=PARAMS,
        cost_estimate=pl.CostEstimate(flops=10**6, bytes_accessed=10**7, transcendentals=0),
        name="seal",
    )(seal_state, seal_blocks, seal_scales, seal_volume, from_low, from_high)

    answers = pl.pallas_call(
        answer_kernel,
        in_specs=[VMEM] * 2,
        out_specs=VMEM,
        out_shape=shape((groups * 24, LANES), F32),
        compiler_params=PARAMS,
        name="answers",
    )(seal_state, arrived)
    returned = exchange(answers, sectors, 12)

    near = lambda number, at: pl.BlockSpec((1, 36, 16, LANES), lambda i: (number, 0, at, 0))
    deep = 4
    halo_operands = halos if halos else (seal_scales[0, :1], seal_scales[0, :1])
    seal_result = pl.pallas_call(
        functools.partial(seal_add_kernel, halo_rows, sectors),
        grid=(1,),
        in_specs=[whole(seal_part), whole(arrived), near(1, 0), near(2, seal_rows // 16 - 1), whole(seal_scales)]
        + [whole(h) for h in halo_operands],
        out_specs=pl.BlockSpec(seal_part.shape, lambda i: (0, 0, 0)),
        out_shape=shape(seal_state.shape, F32),
        scratch_shapes=[
            pltpu.VMEM((12 * seal_rows, deep * LANES), BF16),
            pltpu.VMEM((WIDE, deep * LANES), BF16),
            pltpu.VMEM((12 * seal_rows, WIDE), F32),
        ],
        compiler_params=PARAMS,
        cost_estimate=pl.CostEstimate(flops=10**6, bytes_accessed=10**7, transcendentals=0),
        name="seal_add",
    )(seal_part, arrived, seal_blocks, seal_blocks, seal_scales, *halo_operands)

    cavity_result = pl.pallas_call(
        cavity_add_kernel,
        in_specs=[VMEM] * 6,
        out_specs=VMEM,
        out_shape=shape((12, cells), F32),
        scratch_shapes=[
            pltpu.VMEM((2 * rows, LANES), F32),
            pltpu.VMEM((32 * cells // WIDE, count), BF16),
            pltpu.VMEM((WIDE, count), BF16),
        ],
        compiler_params=PARAMS,
        name="cavity_add",
    )(cavity_part, returned, slots, cavity_index, link_rows, link_scales)
    return seal_result, cavity_result


def solution(mesh):
    return jax.shard_map(
        on_device,
        mesh=mesh,
        in_specs=(
            P(None, "circ", "axial"),
            P(None, None, "circ", "axial"),
            P(None, "circ", "axial"),
            P("circ", "axial"),
            P(None, ("circ", "axial")),
            P(None, None, ("circ", "axial")),
            P(None, ("circ", "axial")),
            P(None, ("circ", "axial")),
            P(("circ", "axial")),
            P(("circ", "axial"), None),
            P(("circ", "axial")),
            P(("circ", "axial")),
            P(None, None, ("circ", "axial")),
            P(None, ("circ", "axial")),
        ),
        out_specs=(P(None, "circ", "axial"), P(None, ("circ", "axial"))),
        check_vma=False,
    )
```

profile of v0, /device:TPU:1, one launch (start us, length us, event | category | flops | bytes accessed | tf_op | source)
XLA Modules:
  0.0 62.1 jit_solution(1531837746294957286)
XLA Ops:
  0.6 0.0 copy-start
  0.6 0.0 copy-start.1
  0.7 1.1 %copy-done.1 = f32[12,64,128]{2,1,0:T(8,128)S(1)} copy-done((f32[12,64,128]{2,1,0:T(8,128)S(1)}, f32[12,64,128]{2,1,0:T(8,128)}, u32[]{:S(2)}) %copy-start.1) | copy-done | bytes 393240
  1.8 0.0 copy-start.4
  1.8 1.0 %copy-done.4 = bf16[2,36,2048]{2,0,1:T(2,128)(2,1)S(1)} copy-done((bf16[2,36,2048]{2,0,1:T(2,128)(2,1)S(1)}, bf16[2,36,2048]{2,0,1:T(2,128)(2,1)}, u32[]{:S(2)}) %copy-start.4) | copy-done | bytes 294936
  2.8 0.0 copy-start.11
  2.8 0.8 %copy-done.11 = f32[12,1024]{1,0:T(8,128)S(1)} copy-done((f32[12,1024]{1,0:T(8,128)S(1)}, f32[12,1024]{1,0:T(8,128)}, u32[]{:S(2)}) %copy-start.11) | copy-done | bytes 49176
  3.6 0.7 %copy-done.13 = f32[2,2048]{1,0:T(2,128)S(1)} copy-done((f32[2,2048]{1,0:T(2,128)S(1)}, f32[2,2048]{1,0:T(2,128)}, u32[]{:S(2)}) %copy-start.13) | copy-done | bytes 16408
  4.3 0.7 %copy-done.16 = s32[2048]{0:T(1024)S(1)} copy-done((s32[2048]{0:T(1024)S(1)}, s32[2048]{0:T(1024)}, u32[]{:S(2)}) %copy-start.16) | copy-done | bytes 8216
  5.0 0.7 %copy-done.20 = s32[2048,1]{0,1:T(1,128)S(1)} copy-done((s32[2048,1]{0,1:T(1,128)S(1)}, s32[2048,1]{0,1:T(1,128)}, u32[]{:S(2)}) %copy-start.20) | copy-done | bytes 8216
  5.7 0.7 %copy-done.21 = s32[2048]{0:T(1024)S(1)} copy-done((s32[2048]{0:T(1024)S(1)}, s32[2048]{0:T(1024)}, u32[]{:S(2)}) %copy-start.21) | copy-done | bytes 8216
  6.4 1.5 %interface.1 = (f32[512,128]{1,0:T(8,128)S(1)}, s32[16,128]{1,0:T(8,128)S(1)}) custom-call(s32[16,128]{1,0:T(8,128)S(1)} %bitcast.20, s32[16,128]{1,0:T(8,128)S(1)} %bitcast.21, s32[16,128]{1,0:T(8,128)S(1)} %bitcast.18, f32[12,1024]{1,0:T(8,128)S(1)} %copy-done.11, bf16[36,2,2048]{2,1,0:T(2,128)(2,1)S(1)} %bitcast.13, f32[2,2048]{1,0:T(2,128)S(1)} %copy-done.13, ...), custom_call_target="tpu_custom_call" | custom-call | tf_op jit(solution)/shard_map/interface/pallas_call | solution.py:386
  7.9 13.5 %all_to_all.10 = f32[8,64,128]{2,1,0:T(8,128)S(1)} all-to-all(f32[8,64,128]{2,1,0:T(8,128)S(1)} %bitcast.17), channel_id=1, replica_groups=mesh['circ'=8,'axial'=4] {'circ'}, dimensions={0} | all-to-all | bytes 524288 | tf_op jit(solution)/shard_map/all_to_all | solution.py:343
  21.4 9.1 %answers.1 = f32[384,128]{1,0:T(8,128)S(1)} custom-call(f32[12,64,128]{2,1,0:T(8,128)S(1)} %copy-done.1, f32[512,128]{1,0:T(8,128)S(1)} %bitcast.11), custom_call_target="tpu_custom_call" | custom-call | tf_op jit(solution)/shard_map/answers/pallas_call | solution.py:466
  30.5 0.0 copy-start.6
  30.5 0.7 %copy-done.6 = f32[384,128]{1,0:T(8,128)} copy-done((f32[384,128]{1,0:T(8,128)}, f32[384,128]{1,0:T(8,128)S(1)}, u32[]{:S(2)}) %copy-start.6) | copy-done | bytes 196632
  31.1 4.8 %all-to-all-start.1 = ((f32[8,48,128]{2,1,0:T(8,128)}), f32[8,48,128]{2,1,0:T(8,128)S(1)}, u32[]{:S(2)}, u32[]{:S(2)}) async-start(f32[8,48,128]{2,1,0:T(8,128)} %bitcast.16), calls=%async_computation.1 | async-start | bytes 393216 | tf_op jit(solution)/shard_map/all_to_all | solution.py:343
  35.9 1.0 %copy-done.2 = f32[12,64,128]{2,1,0:T(8,128)S(1)} copy-done((f32[12,64,128]{2,1,0:T(8,128)S(1)}, f32[12,64,128]{2,1,0:T(8,128)}, u32[]{:S(2)}) %copy-start.2) | copy-done | bytes 393240
  36.9 0.3 faces.1
  37.2 4.3 %collective-permute-start = (f32[64,128]{1,0:T(8,128)S(1)}, f32[64,128]{1,0:T(8,128)S(1)}, u32[]{:S(2)}, u32[]{:S(2)}) collective-permute-start(f32[64,128]{1,0:T(8,128)S(1)} %faces.1), channel_id=1, source_target_pairs={{0,1},{1,2},{2,3},{4,5},{5,6},{6,7},{8,9},{9,10},{10,11},{12,13},{... | collective-permute-start | bytes 98312 | tf_op jit(solution)/shard_map/ppermute | solution.py:415
  41.5 1.9 %collective-permute-start.1 = (f32[64,128]{1,0:T(8,128)S(1)}, f32[64,128]{1,0:T(8,128)S(1)}, u32[]{:S(2)}, u32[]{:S(2)}) collective-permute-start(f32[64,128]{1,0:T(8,128)S(1)} %faces.1), channel_id=1, source_target_pairs={{1,0},{2,1},{3,2},{5,4},{6,5},{7,6},{9,8},{10,9},{11,10},{13,12},{... | collective-permute-start | bytes 98312 | tf_op jit(solution)/shard_map/ppermute | solution.py:416
  43.5 0.7 %slice_bitcast_fusion.halo_low.halo_high = f32[1,128]{1,0:T(1,128)S(1)} fusion(f32[5,64,128]{2,1,0:T(8,128)} %scales.7), kind=kLoop, calls=%fused_computation | loop fusion | bytes 1024 | tf_op jit(solution)/shard_map/squeeze | solution.py:478
  44.2 0.0 copy-done.19
  44.2 0.0 copy-done.22
  44.2 1.0 %copy-done.5 = bf16[2,36,2048]{2,0,1:T(2,128)(2,1)S(1)} copy-done((bf16[2,36,2048]{2,0,1:T(2,128)(2,1)S(1)}, bf16[2,36,2048]{2,0,1:T(2,128)(2,1)}, u32[]{:S(2)}) %copy-start.5) | copy-done | bytes 294936
  45.1 1.0 %copy-done.8 = bf16[5,36,1024]{2,1,0:T(8,128)(2,1)S(1)} copy-done((bf16[5,36,1024]{2,1,0:T(8,128)(2,1)S(1)}, bf16[5,36,1024]{2,1,0:T(8,128)(2,1)}, u32[]{:S(2)}) %copy-start.8) | copy-done | bytes 368664
  46.1 0.8 %copy-done.12 = f32[12,1024]{1,0:T(8,128)S(1)} copy-done((f32[12,1024]{1,0:T(8,128)S(1)}, f32[12,1024]{1,0:T(8,128)}, u32[]{:S(2)}) %copy-start.12) | copy-done | bytes 49176
  47.0 0.8 %copy-done.18 = f32[5,1024]{1,0:T(8,128)S(1)} copy-done((f32[5,1024]{1,0:T(8,128)S(1)}, f32[5,1024]{1,0:T(8,128)}, u32[]{:S(2)}) %copy-start.18) | copy-done | bytes 20504
  47.7 0.7 %cavity.1 = (f32[12,1024]{1,0:T(8,128)S(1)}, f32[576,128]{1,0:T(8,128)S(1)}) custom-call(f32[12,1024]{1,0:T(8,128)S(1)} %copy-done.12, bf16[5,36,1024]{2,1,0:T(8,128)(2,1)S(1)} %copy-done.8, f32[5,1024]{1,0:T(8,128)S(1)} %copy-done.18, s32[4,1024]{1,0:T(4,128)S(1)} %copy-done.19, f32[8,128]{1,0:T(8,128)S(1)} %bitcast.22, bf16[36,2,2048]{2,1,0:T(2,128)(2,1)S(1)} %bitcast.14), custom_call_target="tpu_custom_call" | custom-call | flops 1000000 | bytes 10000000 | tf_op jit(solution)/shard_map/cavity/pallas_call | solution.py:426
  48.5 0.0 copy-start.9
  48.5 0.7 %copy-done.9 = f32[576,128]{1,0:T(8,128)} copy-done((f32[576,128]{1,0:T(8,128)}, f32[576,128]{1,0:T(8,128)S(1)}, u32[]{:S(2)}) %copy-start.9) | copy-done | bytes 294936
  49.2 0.0 collective-permute-done.from_low
  49.2 0.0 collective-permute-done.1.from_high
  49.2 0.0 copy-done
  49.2 0.0 copy-start.3
  49.2 1.0 %copy-done.3 = f32[12,64,128]{2,1,0:T(8,128)S(1)} copy-done((f32[12,64,128]{2,1,0:T(8,128)S(1)}, f32[12,64,128]{2,1,0:T(8,128)}, u32[]{:S(2)}) %copy-start.3) | copy-done | bytes 393240
  50.2 0.9 %copy-done.7 = f32[5,64,128]{2,1,0:T(8,128)S(1)} copy-done((f32[5,64,128]{2,1,0:T(8,128)S(1)}, f32[5,64,128]{2,1,0:T(8,128)}, u32[]{:S(2)}) %copy-start.7) | copy-done | bytes 163864
  51.1 0.8 %copy-done.15 = f32[64,128]{1,0:T(8,128)S(1)} copy-done((f32[64,128]{1,0:T(8,128)S(1)}, f32[64,128]{1,0:T(8,128)}, u32[]{:S(2)}) %copy-start.15) | copy-done | bytes 32792
  51.9 2.4 %seal.1.part = f32[12,64,128]{2,1,0:T(8,128)S(1)} custom-call(f32[12,64,128]{2,1,0:T(8,128)S(1)} %copy-done.3, bf16[5,36,64,128]{3,2,1,0:T(8,128)(2,1)S(1)} %copy-done, f32[5,64,128]{2,1,0:T(8,128)S(1)} %copy-done.7, f32[64,128]{1,0:T(8,128)S(1)} %copy-done.15, f32[64,128]{1,0:T(8,128)S(1)} %collective-permute-done.from_low, ...), custom_call_target="tpu_custom_call" | custom-call | flops 1000000 | bytes 10000000 | tf_op jit(solution)/shard_map/seal/pallas_call | solution.py:444
  54.3 0.0 copy-start.14
  54.3 0.0 copy-start.17
  54.3 4.6 %seal_add.1 = f32[12,64,128]{2,1,0:T(8,128)} custom-call(f32[12,64,128]{2,1,0:T(8,128)S(1)} %seal.1.part, f32[512,128]{1,0:T(8,128)S(1)} %bitcast.12, bf16[5,36,64,128]{3,2,1,0:T(8,128)(2,1)S(1)} %copy-done, bf16[5,36,64,128]{3,2,1,0:T(8,128)(2,1)S(1)} %copy-done, f32[5,64,128]{2,1,0:T(8,128)S(1)} %copy-done.7, ...), custom_call_target="tpu_custom_call" | custom-call | flops 1000000 | bytes 10000000 | tf_op jit(solution)/shard_map/seal_add/pallas_call | solution.py:479
  58.9 0.0 all-to-all-done.1
  58.9 0.0 copy-done.14
  58.9 0.0 copy-done.17
  58.9 0.0 copy-start.10
  58.9 1.0 %copy-done.10 = f32[576,128]{1,0:T(8,128)S(1)} copy-done((f32[576,128]{1,0:T(8,128)S(1)}, f32[576,128]{1,0:T(8,128)}, u32[]{:S(2)}) %copy-start.10) | copy-done | bytes 294936
  59.8 2.3 %cavity_add.1 = f32[12,1024]{1,0:T(8,128)} custom-call(f32[12,1024]{1,0:T(8,128)S(1)} %get-tuple-element.7.part, f32[384,128]{1,0:T(8,128)S(1)} %bitcast.15, s32[16,128]{1,0:T(8,128)S(1)} %get-tuple-element.8.slots, s32[16,128]{1,0:T(8,128)S(1)} %bitcast.19, f32[576,128]{1,0:T(8,128)S(1)} %copy-done.10, f32[2,2048]{1,0:T(2,128)S(1)} %copy-done.14), custom_call_target="tpu_custom_call" | custom-call | tf_op jit(solution)/shard_map/cavity_add/pallas_call | solution.py:496
  (13 shorter events, 0.0 us)
Async XLA Ops:
  0.6 48.6 %copy-start = (bf16[5,36,64,128]{3,2,1,0:T(8,128)(2,1)S(1)}, bf16[5,36,64,128]{3,2,1,0:T(8,128)(2,1)}, u32[]{:S(2)}) copy-start(bf16[5,36,64,128]{3,2,1,0:T(8,128)(2,1)} %blocks_high.1) | copy-start | bytes 8847364
  0.6 1.1 %copy-start.1 = (f32[12,64,128]{2,1,0:T(8,128)S(1)}, f32[12,64,128]{2,1,0:T(8,128)}, u32[]{:S(2)}) copy-start(f32[12,64,128]{2,1,0:T(8,128)} %state.9) | copy-start | bytes 1179652
  1.8 1.0 %copy-start.4 = (bf16[2,36,2048]{2,0,1:T(2,128)(2,1)S(1)}, bf16[2,36,2048]{2,0,1:T(2,128)(2,1)}, u32[]{:S(2)}) copy-start(bf16[2,36,2048]{2,0,1:T(2,128)(2,1)} %param.26) | copy-start | bytes 884740
  2.8 0.8 %copy-start.11 = (f32[12,1024]{1,0:T(8,128)S(1)}, f32[12,1024]{1,0:T(8,128)}, u32[]{:S(2)}) copy-start(f32[12,1024]{1,0:T(8,128)} %state.8) | copy-start | bytes 147460
  3.6 0.7 %copy-start.13 = (f32[2,2048]{1,0:T(2,128)S(1)}, f32[2,2048]{1,0:T(2,128)}, u32[]{:S(2)}) copy-start(f32[2,2048]{1,0:T(2,128)} %scales.9) | copy-start | bytes 49156
  4.3 0.7 %copy-start.16 = (s32[2048]{0:T(1024)S(1)}, s32[2048]{0:T(1024)}, u32[]{:S(2)}) copy-start(s32[2048]{0:T(1024)} %param.25) | copy-start | bytes 24580
  5.0 0.7 %copy-start.20 = (s32[2048,1]{0,1:T(1,128)S(1)}, s32[2048,1]{0,1:T(1,128)}, u32[]{:S(2)}) copy-start(s32[2048,1]{0,1:T(1,128)} %param.23) | copy-start | bytes 24580
  5.7 0.7 %copy-start.21 = (s32[2048]{0:T(1024)S(1)}, s32[2048]{0:T(1024)}, u32[]{:S(2)}) copy-start(s32[2048]{0:T(1024)} %param.24) | copy-start | bytes 24580
  6.4 37.8 %copy-start.19 = (s32[4,1024]{1,0:T(4,128)S(1)}, s32[4,1024]{1,0:T(4,128)}, u32[]{:S(2)}) copy-start(s32[4,1024]{1,0:T(4,128)} %links.1) | copy-start | bytes 49156
  6.4 37.8 %copy-start.22 = (f32[1024]{0:T(1024)S(1)}, f32[1024]{0:T(1024)}, u32[]{:S(2)}) copy-start(f32[1024]{0:T(1024)} %param.22) | copy-start | bytes 12292
  30.5 0.7 %copy-start.6 = (f32[384,128]{1,0:T(8,128)}, f32[384,128]{1,0:T(8,128)S(1)}, u32[]{:S(2)}) copy-start(f32[384,128]{1,0:T(8,128)S(1)} %answers.1) | copy-start | bytes 589828
  31.1 27.7 %all-to-all-start.1 = ((f32[8,48,128]{2,1,0:T(8,128)}), f32[8,48,128]{2,1,0:T(8,128)S(1)}, u32[]{:S(2)}, u32[]{:S(2)}) async-start(f32[8,48,128]{2,1,0:T(8,128)} %bitcast.16), calls=%async_computation.1 | async-start | bytes 393216 | tf_op jit(solution)/shard_map/all_to_all | solution.py:343
  35.9 1.0 %copy-start.2 = (f32[12,64,128]{2,1,0:T(8,128)S(1)}, f32[12,64,128]{2,1,0:T(8,128)}, u32[]{:S(2)}) copy-start(f32[12,64,128]{2,1,0:T(8,128)} %state.9) | copy-start | bytes 1179652
  37.2 12.0 %collective-permute-start = (f32[64,128]{1,0:T(8,128)S(1)}, f32[64,128]{1,0:T(8,128)S(1)}, u32[]{:S(2)}, u32[]{:S(2)}) collective-permute-start(f32[64,128]{1,0:T(8,128)S(1)} %faces.1), channel_id=1, source_target_pairs={{0,1},{1,2},{2,3},{4,5},{5,6},{6,7},{8,9},{9,10},{10,11},{12,13},{... | collective-permute-start | bytes 98312 | tf_op jit(solution)/shard_map/ppermute | solution.py:415
  41.5 7.7 %collective-permute-start.1 = (f32[64,128]{1,0:T(8,128)S(1)}, f32[64,128]{1,0:T(8,128)S(1)}, u32[]{:S(2)}, u32[]{:S(2)}) collective-permute-start(f32[64,128]{1,0:T(8,128)S(1)} %faces.1), channel_id=1, source_target_pairs={{1,0},{2,1},{3,2},{5,4},{6,5},{7,6},{9,8},{10,9},{11,10},{13,12},{... | collective-permute-start | bytes 98312 | tf_op jit(solution)/shard_map/ppermute | solution.py:416
  44.2 1.0 %copy-start.5 = (bf16[2,36,2048]{2,0,1:T(2,128)(2,1)S(1)}, bf16[2,36,2048]{2,0,1:T(2,128)(2,1)}, u32[]{:S(2)}) copy-start(bf16[2,36,2048]{2,0,1:T(2,128)(2,1)} %param.26) | copy-start | bytes 884740
  45.1 1.0 %copy-start.8 = (bf16[5,36,1024]{2,1,0:T(8,128)(2,1)S(1)}, bf16[5,36,1024]{2,1,0:T(8,128)(2,1)}, u32[]{:S(2)}) copy-start(bf16[5,36,1024]{2,1,0:T(8,128)(2,1)} %blocks.3) | copy-start | bytes 1105924
  46.1 0.8 %copy-start.12 = (f32[12,1024]{1,0:T(8,128)S(1)}, f32[12,1024]{1,0:T(8,128)}, u32[]{:S(2)}) copy-start(f32[12,1024]{1,0:T(8,128)} %state.8) | copy-start | bytes 147460
  47.0 0.8 %copy-start.18 = (f32[5,1024]{1,0:T(8,128)S(1)}, f32[5,1024]{1,0:T(8,128)}, u32[]{:S(2)}) copy-start(f32[5,1024]{1,0:T(8,128)} %scales.8) | copy-start | bytes 61444
  48.5 0.7 %copy-start.9 = (f32[576,128]{1,0:T(8,128)}, f32[576,128]{1,0:T(8,128)S(1)}, u32[]{:S(2)}) copy-start(f32[576,128]{1,0:T(8,128)S(1)} %get-tuple-element.9.link_rows) | copy-start | bytes 884740
  49.2 1.0 %copy-start.3 = (f32[12,64,128]{2,1,0:T(8,128)S(1)}, f32[12,64,128]{2,1,0:T(8,128)}, u32[]{:S(2)}) copy-start(f32[12,64,128]{2,1,0:T(8,128)} %state.9) | copy-start | bytes 1179652
  50.2 0.9 %copy-start.7 = (f32[5,64,128]{2,1,0:T(8,128)S(1)}, f32[5,64,128]{2,1,0:T(8,128)}, u32[]{:S(2)}) copy-start(f32[5,64,128]{2,1,0:T(8,128)} %scales.7) | copy-start | bytes 491524
  51.1 0.8 %copy-start.15 = (f32[64,128]{1,0:T(8,128)S(1)}, f32[64,128]{1,0:T(8,128)}, u32[]{:S(2)}) copy-start(f32[64,128]{1,0:T(8,128)} %volume.1) | copy-start | bytes 98308
  54.3 4.6 %copy-start.14 = (f32[2,2048]{1,0:T(2,128)S(1)}, f32[2,2048]{1,0:T(2,128)}, u32[]{:S(2)}) copy-start(f32[2,2048]{1,0:T(2,128)} %scales.9) | copy-start | bytes 49156
  54.3 4.6 %copy-start.17 = (s32[2048]{0:T(1024)S(1)}, s32[2048]{0:T(1024)}, u32[]{:S(2)}) copy-start(s32[2048]{0:T(1024)} %param.25) | copy-start | bytes 24580
  58.9 1.0 %copy-start.10 = (f32[576,128]{1,0:T(8,128)S(1)}, f32[576,128]{1,0:T(8,128)}, u32[]{:S(2)}) copy-start(f32[576,128]{1,0:T(8,128)} %copy-done.9) | copy-start | bytes 884740
where the time goes:
time: 63.1 us; the launch traced here: 62.1 us
  Pallas kernels  20.8 us (33%)
  local copies, waits for them, and re-layouts  16 us (25%)
  blocking collectives  13.5 us (21%)
  starting transfers between devices  11.1 us (18%)
  between operations  0.78 us (1%)
    unnamed x46, local copies, waits for them, and re-layouts  15.3 us
    all_to_all x1, blocking collectives, exchange(): lax.all_to_all(shaped, 'circ', split_axis=0, concat_axis=0, tiled=True)  13.5 us
    pallas_call x1, Pallas kernels, on_device(): pl.pallas_call(answer_kernel, in_specs=[VMEM] * 2, out_specs=VMEM, out_sh...  9.05 us
    all_to_all x1, starting transfers between devices, exchange(): lax.all_to_all(shaped, 'circ', split_axis=0, concat_axis=0, tiled=True)  4.79 us
    pallas_call x1, Pallas kernels, on_device(): pl.pallas_call(functools.partial(seal_add_kernel, halo_rows, sectors), gr...  4.56 us
    ppermute x1, starting transfers between devices, on_device(): lax.ppermute(faces, 'axial', [(i, i + 1) for i in range(segments - 1)])  4.34 us
    pallas_call x1, Pallas kernels, on_device(): pl.pallas_call(functools.partial(seal_kernel, step_rows), grid=(seal_rows...  2.39 us
    pallas_call x1, Pallas kernels, on_device(): pl.pallas_call(cavity_add_kernel, in_specs=[VMEM] * 6, out_specs=VMEM, ou...  2.3 us
  transfers between devices with their start and end apart: 3, of which 0 were waited for; matrix products, arithmetic and copies ran while one was open for 1% of the time, Pallas kernels for 13%

commit v1 on v0

--- a/solution.py
+++ b/solution.py
@@ -10,8 +10,9 @@
 F32, BF16, I32 = jnp.float32, jnp.bfloat16, jnp.int32
 LANES = 128
 WIDE = 256
-PARAMS = pltpu.CompilerParams(vmem_limit_bytes=40 * 1024 * 1024)
+PARAMS = pltpu.CompilerParams(vmem_limit_bytes=16 * 1024 * 1024)
 VMEM = pl.BlockSpec(memory_space=pltpu.VMEM)
+HBM = pl.BlockSpec(memory_space=pltpu.HBM)
 
 
 def iota(shape, axis):
@@ -21,6 +22,10 @@
 def lane_take(row, index):
     table = jnp.broadcast_to(row, index.shape)
     return jnp.take_along_axis(table, index, axis=1, mode="promise_in_bounds")
+
+
+def one_hot(index):
+    return jnp.where(iota((WIDE, index.shape[1]), 0) == index, 1.0, 0.0).astype(BF16)
 
 
 def halves(value):
@@ -54,9 +59,25 @@
 
 
 def interface_kernel(
-    sectors, halo_rows, owner, seal_index, cavity_index, state, blocks, scales, first, last,
-    send, slots, block_rows, scale_rows, state_rows, left, right,
+    sectors, halo_rows, owner_hbm, seal_index_hbm, cavity_index_hbm, state_hbm, blocks_hbm,
+    scales_hbm, seal_hbm, send, slots, block_rows, scale_rows, state_rows, left, right,
+    owner, seal_index, cavity_index, state, blocks, scales, first, last, arrivals,
 ):
+    last_row = seal_hbm.shape[1]
+    loads = start_loads(
+        (
+            (owner_hbm, owner),
+            (blocks_hbm, blocks),
+            (scales_hbm, scales),
+            (state_hbm, state),
+            (cavity_index_hbm, cavity_index),
+            (seal_index_hbm, seal_index),
+            (seal_hbm.at[:, 0:8, :], first),
+            (seal_hbm.at[:, last_row - 8 : last_row, :], last),
+        ),
+        arrivals,
+    )
+    loads[0].wait()
     rows = owner.shape[0]
     capacity = 2 * rows * LANES // sectors
     sector_id = iota((sectors, LANES), 0)
@@ -73,6 +94,8 @@
         place = jnp.sum(hot[c] * (prefix[part] + offset), axis=0, keepdims=True)
         slots[c : c + 1, :] = owner[c : c + 1, :] * capacity + place.astype(I32)
         offset = offset + totals[part]
+    for load in loads[1:]:
+        load.wait()
     for entry in range(36):
         both = blocks[entry].astype(F32)
         for c in range(rows):
@@ -99,9 +122,7 @@
     for c in range(rows):
         slot = slots[c : c + 1, :]
         cols = slice(c * LANES, (c + 1) * LANES)
-        right[:, cols] = jnp.where(
-            iota((WIDE, LANES), 0) == (slot & (WIDE - 1)), 1.0, 0.0
-        ).astype(BF16)
+        right[:, cols] = one_hot(slot & (WIDE - 1))
         here = iota((groups, LANES), 0) == (slot >> 8)
         for number, part in enumerate(parts):
             left[number * groups : (number + 1) * groups, cols] = jnp.where(
@@ -127,67 +148,120 @@
                 send[pl.ds(base + (f // 3) * 16 + 13 + f % 3, 1), :] = edge[f, row : row + 1, :]
 
 
-def face_kernel(state, faces):
+def start_loads(pairs, arrivals):
+    loads = [
+        pltpu.make_async_copy(source, target, arrivals.at[number])
+        for number, (source, target) in enumerate(pairs)
+    ]
+    for load in loads:
+        load.start()
+    return loads
+
+
+def face_kernel(state_hbm, faces, state, table, arrivals):
+    (load,) = start_loads([(state_hbm, state)], arrivals)
+    load.wait()
     lane = iota(faces.shape, 1)
+    half_rows = faces.shape[0] // 2
     total = jnp.zeros(faces.shape, F32)
     for f in range(12):
-        total = jnp.where(lane == f, pltpu.roll(state[f], f + 1, 1), total)
-        total = jnp.where(lane == 16 + f, pltpu.roll(state[f], 16 + f, 1), total)
+        own = state[f]
+        total = jnp.where(lane == f, pltpu.roll(own, f + 1, 1), total)
+        total = jnp.where(lane == 16 + f, pltpu.roll(own, 16 + f, 1), total)
+        at = pl.ds(f * half_rows, half_rows)
+        for half in range(2):
+            high, low = halves(own[half * half_rows : (half + 1) * half_rows, :])
+            table[0, at, half * LANES : (half + 1) * LANES] = high.astype(BF16)
+            table[1, at, half * LANES : (half + 1) * LANES] = low.astype(BF16)
     faces[...] = total
 
 
-def seal_kernel(step_rows, state, blocks, scales, volume, from_low, from_high, out, beside, along):
+def seal_kernel(step_rows, state, blocks, scales, volume, inner, outer, out, edges, beside, along):
     rows = state.shape[1]
-
-    @pl.when(pl.program_id(0) == 0)
-    def _():
-        lane = iota((rows, LANES), 1)
-        low, high = from_low[...], from_high[...]
+    lane = iota((rows, LANES), 1)
+    odd = lax.rem(lax.axis_index("axial"), 2) == 1
+    low = jnp.where(odd, inner[...], outer[...])
+    high = jnp.where(odd, outer[...], inner[...])
+    for f in range(12):
+        beside[0, f, 1:rows, :] = state[f, 0 : rows - 1, :]
+        beside[0, f, 0:1, :] = jnp.zeros((1, LANES), F32)
+        beside[1, f, 0 : rows - 1, :] = state[f, 1:rows, :]
+        beside[1, f, rows - 1 : rows, :] = jnp.zeros((1, LANES), F32)
+        own = state[f]
+        edge = pltpu.roll(low, (LANES - f) % LANES, 1)
+        along[0, f] = jnp.where(lane == 0, edge, pltpu.roll(own, 1, 1))
+        edge = pltpu.roll(high, LANES - 1 - 16 - f, 1)
+        along[1, f] = jnp.where(lane == LANES - 1, edge, pltpu.roll(own, LANES - 1, 1))
+
+    def add_rows(step, carry):
+        here = pl.ds(pl.multiple_of(step * step_rows, step_rows), step_rows)
+        own = [state[f, here, :] for f in range(12)]
+        totals = whirl(own, volume[here, :])
+        for number in range(5):
+            if number == 0:
+                vector = own
+            else:
+                source = beside if number < 3 else along
+                vector = [source[(number - 1) % 2, f, here, :] for f in range(12)]
+            totals = product_into(
+                totals, lambda e: blocks[number, e, here, :].astype(F32), scales[number, here, :], vector
+            )
         for f in range(12):
-            beside[0, f, 1:rows, :] = state[f, 0 : rows - 1, :]
-            beside[0, f, 0:1, :] = jnp.zeros((1, LANES), F32)
-            beside[1, f, 0 : rows - 1, :] = state[f, 1:rows, :]
-            beside[1, f, rows - 1 : rows, :] = jnp.zeros((1, LANES), F32)
-            own = state[f]
-            edge = pltpu.roll(low, (LANES - f) % LANES, 1)
-            along[0, f] = jnp.where(lane == 0, edge, pltpu.roll(own, 1, 1))
-            edge = pltpu.roll(high, LANES - 1 - 16 - f, 1)
-            along[1, f] = jnp.where(lane == LANES - 1, edge, pltpu.roll(own, LANES - 1, 1))
-
-    start = pl.multiple_of(pl.program_id(0) * step_rows, step_rows)
-    here = pl.ds(start, step_rows)
-    own = [state[f, here, :] for f in range(12)]
-    totals = whirl(own, volume[here, :])
-    for number in range(5):
-        if number == 0:
-            vector = own
-        else:
-            source = beside if number < 3 else along
-            vector = [source[(number - 1) % 2, f, here, :] for f in range(12)]
-        totals = product_into(
-            totals, lambda e: blocks[number, e].astype(F32), scales[number, here, :], vector
+            out[f, here, :] = totals[f]
+        return carry
+
+    lax.fori_loop(0, rows // step_rows, add_rows, 0)
+    for number, near, at in ((1, 0, 0), (2, rows - 16, 15)):
+        first = (number - 1) * 40
+        for e in range(36):
+            tile = blocks[number, e, near : near + 16, :].astype(F32)
+            edges[first + e : first + e + 1, :] = tile[at : at + 1, :]
+        edges[first + 36 : first + 37, :] = scales[number, near + at : near + at + 1, :]
+        edges[first + 37 : first + 40, :] = jnp.zeros((3, LANES), F32)
+
+
+def pick(table, hot, here):
+    found = jnp.dot(table[0], hot, preferred_element_type=F32)
+    found = found + jnp.dot(table[1], hot, preferred_element_type=F32)
+    bands = here.shape[0]
+    return [
+        jnp.sum(jnp.where(here, found[f * bands : (f + 1) * bands, :], 0.0), axis=0, keepdims=True)
+        for f in range(12)
+    ]
+
+
+def answer_kernel(width, table, arrived, send_hbm, send, sent):
+    chunks = arrived.shape[0] // 16
+    half_rows = table.shape[1] // 12
+    copies = []
+    for base in range(0, chunks, width):
+        cell = jnp.concatenate(
+            [arrived[g * 16 + 12 : g * 16 + 13, :] for g in range(base, base + width)], axis=1
+        ).astype(I32)
+        row = cell >> 7
+        upper = row >= half_rows
+        index = (cell & (LANES - 1)) + jnp.where(upper, LANES, 0)
+        row = row - jnp.where(upper, half_rows, 0)
+        here = iota((half_rows, width * LANES), 0) == row
+        value = pick(table, one_hot(index), here)
+        for f in range(12):
+            for part in range(width):
+                at = (base + part) * 12 + f
+                send[at : at + 1, :] = value[f][:, part * LANES : (part + 1) * LANES]
+        done = pl.ds(base * 12, width * 12)
+        copies.append(
+            pltpu.make_async_copy(send.at[done, :], send_hbm.at[done, :], sent.at[base // width])
         )
-    for f in range(12):
-        out[f] = totals[f]
-
-
-def answer_kernel(state, arrived, send):
-    chunks = arrived.shape[0] // 16
-    cell = arrived[pl.ds(12, chunks, stride=16), :].astype(I32)
-    lane, high = cell & (LANES - 1), cell >> 7
-    value = [jnp.zeros(cell.shape, F32)] * 12
-    for r in range(state.shape[1]):
-        here = high == r
-        for f in range(12):
-            value[f] = jnp.where(here, lane_take(state[f, r : r + 1, :], lane), value[f])
-    for f in range(12):
-        send[pl.ds(f, chunks, stride=12), :] = value[f]
+        copies[-1].start()
+    for copy in copies:
+        copy.wait()
 
 
 def seal_add_kernel(
-    halo_rows, sectors, part, arrived, blocks_low, blocks_high, scales, halo_low, halo_high,
-    out, left, right, total,
+    halo_rows, sectors, part, arrived, edges, slots, cavity_index,
+    *refs,
 ):
+    *halos, out, slot_hot, cell_hot, left, right, total = refs
     chunks = arrived.shape[0] // 16
     rows = part.shape[1]
     half_rows = rows // 2
@@ -203,7 +277,7 @@
             column = (cell & (LANES - 1)) + jnp.where(row >= half_rows, LANES, 0)
             row = jnp.where(row >= half_rows, row - half_rows, row)
             cols = slice(sub * LANES, (sub + 1) * LANES)
-            right[:, cols] = jnp.where(iota((WIDE, LANES), 0) == column, 1.0, 0.0).astype(BF16)
+            right[:, cols] = one_hot(column)
             here = iota((half_rows, LANES), 0) == row
             for f in range(12):
                 for number, source in enumerate((high, low)):
@@ -216,6 +290,10 @@
         )
         return carry
 
+    for c in range(slots.shape[0]):
+        cols = slice(c * LANES, (c + 1) * LANES)
+        for source, target in ((slots, slot_hot), (cavity_index, cell_hot)):
+            target[:, cols] = one_hot(source[c : c + 1, :] & (WIDE - 1))
     lax.fori_loop(0, chunks // deep, add_chunks, 0)
     for f in range(12):
         added = (
@@ -225,21 +303,20 @@
         out[f, 0:half_rows, :] = part[f, 0:half_rows, :] + added[:, :LANES]
         out[f, half_rows:rows, :] = part[f, half_rows:rows, :] + added[:, LANES:]
     me = lax.axis_index("circ")
-    edge = blocks_low.shape[2]
-    for number, step, halo, blocks in ((1, sectors - 1, halo_low, blocks_low), (2, 1, halo_high, blocks_high)):
+    for number, step in ((1, sectors - 1), (2, 1)):
         if halo_rows:
             base = lax.rem(me + step, sectors) * 64
             vector = [
                 arrived[pl.ds(base + (f // 3) * 16 + 13 + f % 3, 1), :] for f in range(12)
             ]
         else:
-            vector = [halo[f] for f in range(12)]
+            vector = [halos[number - 1][f] for f in range(12)]
         at = 0 if number == 1 else rows - 1
-        inner = 0 if number == 1 else edge - 1
+        first = (number - 1) * 40
         terms = product_into(
             [None] * 12,
-            lambda e: blocks[0, e].astype(F32)[inner : inner + 1, :],
-            scales[number, at : at + 1, :],
+            lambda e: edges[first + e : first + e + 1, :],
+            edges[first + 36 : first + 37, :],
             vector,
         )
         for f in range(12):
@@ -247,9 +324,30 @@
 
 
 def cavity_kernel(
-    state, blocks, scales, links, volume, link_blocks,
-    out, link_rows, state_rows, block_rows, scale_rows, face_rows, out_rows,
+    state_hbm, blocks_hbm, scales_hbm, links_hbm, volume_hbm, link_blocks_hbm, link_scales_hbm,
+    index_hbm, seal_blocks_hbm, seal_scales_hbm, seal_volume_hbm,
+    out, link_rows, link_scale_rows, cavity_index, seal_blocks, seal_scales, seal_volume,
+    state_rows, block_rows, scale_rows, face_rows, out_rows,
+    state, blocks, scales, links, volume, link_blocks, link_scales, arrivals,
 ):
+    loads = start_loads(
+        (
+            (state_hbm, state),
+            (links_hbm, links),
+            (blocks_hbm, blocks),
+            (scales_hbm, scales),
+            (volume_hbm, volume),
+            (link_blocks_hbm, link_blocks),
+            (link_scales_hbm, link_scales),
+            (index_hbm, cavity_index),
+            (seal_scales_hbm, seal_scales),
+            (seal_volume_hbm, seal_volume),
+            (seal_blocks_hbm, seal_blocks),
+        ),
+        arrivals,
+    )
+    for load in loads[:7]:
+        load.wait()
     cells = state.shape[1]
     rows = cells // LANES
     fold_cells(state, state_rows, 12, 0, cells)
@@ -292,22 +390,33 @@
             link_rows[entry * row_count + c : entry * row_count + c + 1, :] = both[
                 1:2, c * LANES : (c + 1) * LANES
             ]
+    fold_cells(link_scales, link_scale_rows, 2, 0, row_count * LANES)
+    for load in loads[7:]:
+        load.wait()
 
 
 def cavity_add_kernel(
-    part, arrived, slots, cavity_index, link_rows, scales, out, scale_rows, left, right
+    width, part, arrived, slots, cavity_index, link_rows, scale_rows, slot_hot, cell_hot,
+    out, left, table, found,
 ):
     rows = slots.shape[0]
     chunks = arrived.shape[0] // 12
-    slot = slots[...]
-    lane, high = slot & (LANES - 1), slot >> 7
-    vector = [jnp.zeros(slot.shape, F32)] * 12
-    for chunk in range(chunks):
-        here = high == chunk
+    groups = chunks // 2
+    for f in range(12):
+        for half in range(2):
+            high, low = halves(arrived[pl.ds(half * 12 + f, groups, stride=24), :])
+            at = pl.ds(f * groups, groups)
+            table[0, at, half * LANES : (half + 1) * LANES] = high.astype(BF16)
+            table[1, at, half * LANES : (half + 1) * LANES] = low.astype(BF16)
+    for base in range(0, rows, width):
+        slot = jnp.concatenate([slots[c : c + 1, :] for c in range(base, base + width)], axis=1)
+        here = iota((groups, width * LANES), 0) == (slot >> 8)
+        value = pick(table, slot_hot[:, base * LANES : (base + width) * LANES], here)
         for f in range(12):
-            row = arrived[chunk * 12 + f : chunk * 12 + f + 1, :]
-            vector[f] = jnp.where(here, lane_take(row, lane), vector[f])
-    fold_cells(scales, scale_rows, 2, 0, rows * LANES)
+            for number in range(width):
+                at = f * rows + base + number
+                found[at : at + 1, :] = value[f][:, number * LANES : (number + 1) * LANES]
+    vector = [found[f * rows : (f + 1) * rows, :] for f in range(12)]
     terms = product_into(
         [None] * 12,
         lambda e: link_rows[e * rows : (e + 1) * rows, :],
@@ -319,7 +428,6 @@
     for c in range(rows):
         cell = cavity_index[c : c + 1, :]
         cols = slice(c * LANES, (c + 1) * LANES)
-        right[:, cols] = jnp.where(iota((WIDE, LANES), 0) == (cell & (WIDE - 1)), 1.0, 0.0).astype(BF16)
         band = cell >> 8
         zero = jnp.zeros((4, LANES), F32)
         tile = jnp.concatenate(
@@ -329,7 +437,7 @@
         for b in range(bands):
             left[b * 32 : (b + 1) * 32, cols] = jnp.where(band == b, tile, 0.0).astype(BF16)
     added = lax.dot_general(
-        left[...], right[...], (((1,), (1,)), ((), ())), preferred_element_type=F32
+        left[...], cell_hot[...], (((1,), (1,)), ((), ())), preferred_element_type=F32
     )
     for b in range(bands):
         cols = slice(b * WIDE, (b + 1) * WIDE)
@@ -380,17 +488,12 @@
     cavity_index = link_cavity.reshape(rows, LANES)
     pair_blocks = link_blocks.transpose(1, 0, 2)
 
-    edge = lambda at: pl.BlockSpec((12, 8, LANES), lambda i: (0, at, 0))
-    whole = lambda a: pl.BlockSpec(a.shape, lambda i: (0,) * len(a.shape))
+    hbm = lambda a: pltpu.with_memory_space_constraint(a, pltpu.HBM)
     head = (owner, seal_index, cavity_index, cavity_state, pair_blocks, link_scales)
     send, slots = pl.pallas_call(
         functools.partial(interface_kernel, sectors, halo_rows),
-        grid=(1,),
-        in_specs=[whole(a) for a in head] + [edge(0), edge(seal_rows // 8 - 1)],
-        out_specs=[
-            pl.BlockSpec((groups * 32, LANES), lambda i: (0, 0)),
-            pl.BlockSpec((rows, LANES), lambda i: (0, 0)),
-        ],
+        in_specs=[HBM] * 7,
+        out_specs=[VMEM, VMEM],
         out_shape=[shape((groups * 32, LANES), F32), shape((rows, LANES), I32)],
         scratch_shapes=[
             pltpu.VMEM((72 * rows, LANES), F32),
@@ -398,22 +501,33 @@
             pltpu.VMEM((12 * cells // LANES, LANES), F32),
             pltpu.VMEM((26 * groups, count), BF16),
             pltpu.VMEM((WIDE, count), BF16),
-        ],
+        ]
+        + [pltpu.VMEM(a.shape, a.dtype) for a in head]
+        + [pltpu.VMEM((12, 8, LANES), F32)] * 2
+        + [pltpu.SemaphoreType.DMA((8,))],
         compiler_params=PARAMS,
         name="interface",
-    )(*head, seal_state, seal_state)
+    )(*[hbm(a) for a in head], hbm(seal_state))
     arrived = exchange(send, sectors, 16)
 
-    faces = pl.pallas_call(
+    faces, state, table = pl.pallas_call(
         face_kernel,
-        in_specs=[VMEM],
-        out_specs=VMEM,
-        out_shape=shape((seal_rows, LANES), F32),
+        in_specs=[HBM],
+        out_specs=[VMEM] * 3,
+        out_shape=[
+            shape((seal_rows, LANES), F32),
+            shape(seal_state.shape, F32),
+            shape((2, 6 * seal_rows, WIDE), BF16),
+        ],
+        scratch_shapes=[pltpu.SemaphoreType.DMA((1,))],
         compiler_params=PARAMS,
         name="faces",
-    )(seal_state)
-    from_low = lax.ppermute(faces, "axial", [(i, i + 1) for i in range(segments - 1)])
-    from_high = lax.ppermute(faces, "axial", [(i + 1, i) for i in range(segments - 1)])
+    )(hbm(seal_state))
+    swaps = lambda begin: [
+        pair for i in range(begin, segments - 1, 2) for pair in ((i, i + 1), (i + 1, i))
+    ]
+    inner = lax.ppermute(faces, "axial", swaps(0))
+    outer = lax.ppermute(faces, "axial", swaps(1))
     if halo_rows:
         halos = ()
     else:
@@ -423,37 +537,38 @@
             lax.ppermute(first, "circ", [((i + 1) % sectors, i) for i in range(sectors)]),
         )
 
-    cavity_part, link_rows = pl.pallas_call(
+    tile = (cavity_state, cavity_blocks, cavity_scales, cavity_links, cavity_volume.reshape(-1, LANES))
+    tile = tile + (pair_blocks, link_scales)
+    kept = (cavity_index, seal_blocks, seal_scales, seal_volume)
+    cavity_part, link_rows, link_scale_rows, kept_index, kept_blocks, kept_scales, kept_volume = pl.pallas_call(
         cavity_kernel,
-        in_specs=[VMEM] * 6,
-        out_specs=[VMEM, VMEM],
-        out_shape=[shape((12, cells), F32), shape((36 * rows, LANES), F32)],
+        in_specs=[HBM] * 11,
+        out_specs=[VMEM] * 7,
+        out_shape=[
+            shape((12, cells), F32),
+            shape((36 * rows, LANES), F32),
+            shape((2 * rows, LANES), F32),
+        ]
+        + [shape(a.shape, a.dtype) for a in kept],
         scratch_shapes=[
             pltpu.VMEM((12 * cells // LANES, LANES), F32),
             pltpu.VMEM((180 * cells // LANES, LANES), F32),
             pltpu.VMEM((5 * cells // LANES, LANES), F32),
             pltpu.VMEM((4 * cells // LANES, LANES), I32),
             pltpu.VMEM((12 * cells // LANES, LANES), F32),
-        ],
+        ]
+        + [pltpu.VMEM(a.shape, a.dtype) for a in tile]
+        + [pltpu.SemaphoreType.DMA((11,))],
         compiler_params=PARAMS,
         cost_estimate=pl.CostEstimate(flops=10**6, bytes_accessed=10**7, transcendentals=0),
         name="cavity",
-    )(cavity_state, cavity_blocks, cavity_scales, cavity_links, cavity_volume.reshape(-1, LANES), pair_blocks)
-
-    step_rows = 16
-    seal_part = pl.pallas_call(
-        functools.partial(seal_kernel, step_rows),
-        grid=(seal_rows // step_rows,),
-        in_specs=[
-            whole(seal_state),
-            pl.BlockSpec((5, 36, step_rows, LANES), lambda i: (0, 0, i, 0)),
-            whole(seal_scales),
-            whole(seal_volume),
-            whole(faces),
-            whole(faces),
-        ],
-        out_specs=pl.BlockSpec((12, step_rows, LANES), lambda i: (0, i, 0)),
-        out_shape=shape(seal_state.shape, F32),
+    )(*[hbm(a) for a in tile + kept])
+
+    seal_part, edges = pl.pallas_call(
+        functools.partial(seal_kernel, 16),
+        in_specs=[VMEM] * 6,
+        out_specs=[VMEM] * 2,
+        out_shape=[shape(seal_state.shape, F32), shape((80, LANES), F32)],
         scratch_shapes=[
             pltpu.VMEM((2,) + seal_state.shape, F32),
             pltpu.VMEM((2,) + seal_state.shape, F32),
@@ -461,28 +576,30 @@
         compiler_params=PARAMS,
         cost_estimate=pl.CostEstimate(flops=10**6, bytes_accessed=10**7, transcendentals=0),
         name="seal",
-    )(seal_state, seal_blocks, seal_scales, seal_volume, from_low, from_high)
-
+    )(state, kept_blocks, kept_scales, kept_volume, inner, outer)
+
+    arrived, seal_part, cavity_part = lax.optimization_barrier((arrived, seal_part, cavity_part))
+    width = 8
     answers = pl.pallas_call(
-        answer_kernel,
+        functools.partial(answer_kernel, width),
         in_specs=[VMEM] * 2,
-        out_specs=VMEM,
-        out_shape=shape((groups * 24, LANES), F32),
+        out_specs=HBM,
+        out_shape=pltpu.HBM((groups * 24, LANES), F32),
+        scratch_shapes=[
+            pltpu.VMEM((groups * 24, LANES), F32),
+            pltpu.SemaphoreType.DMA((2 * groups // width,)),
+        ],
         compiler_params=PARAMS,
         name="answers",
-    )(seal_state, arrived)
+    )(table, arrived)
     returned = exchange(answers, sectors, 12)
 
-    near = lambda number, at: pl.BlockSpec((1, 36, 16, LANES), lambda i: (number, 0, at, 0))
     deep = 4
-    halo_operands = halos if halos else (seal_scales[0, :1], seal_scales[0, :1])
-    seal_result = pl.pallas_call(
+    seal_result, slot_hot, cell_hot = pl.pallas_call(
         functools.partial(seal_add_kernel, halo_rows, sectors),
-        grid=(1,),
-        in_specs=[whole(seal_part), whole(arrived), near(1, 0), near(2, seal_rows // 16 - 1), whole(seal_scales)]
-        + [whole(h) for h in halo_operands],
-        out_specs=pl.BlockSpec(seal_part.shape, lambda i: (0, 0, 0)),
-        out_shape=shape(seal_state.shape, F32),
+        in_specs=[VMEM] * (5 + len(halos)),
+        out_specs=[VMEM] * 3,
+        out_shape=[shape(seal_state.shape, F32)] + [shape((WIDE, count), BF16)] * 2,
         scratch_shapes=[
             pltpu.VMEM((12 * seal_rows, deep * LANES), BF16),
             pltpu.VMEM((WIDE, deep * LANES), BF16),
@@ -491,21 +608,21 @@
         compiler_params=PARAMS,
         cost_estimate=pl.CostEstimate(flops=10**6, bytes_accessed=10**7, transcendentals=0),
         name="seal_add",
-    )(seal_part, arrived, seal_blocks, seal_blocks, seal_scales, *halo_operands)
+    )(seal_part, arrived, edges, slots, kept_index, *halos)
 
     cavity_result = pl.pallas_call(
-        cavity_add_kernel,
-        in_specs=[VMEM] * 6,
+        functools.partial(cavity_add_kernel, 8),
+        in_specs=[VMEM] * 8,
         out_specs=VMEM,
         out_shape=shape((12, cells), F32),
         scratch_shapes=[
-            pltpu.VMEM((2 * rows, LANES), F32),
             pltpu.VMEM((32 * cells // WIDE, count), BF16),
-            pltpu.VMEM((WIDE, count), BF16),
+            pltpu.VMEM((2, 12 * groups, WIDE), BF16),
+            pltpu.VMEM((12 * rows, LANES), F32),
         ],
         compiler_params=PARAMS,
         name="cavity_add",
-    )(cavity_part, returned, slots, cavity_index, link_rows, link_scales)
+    )(cavity_part, returned, slots, kept_index, link_rows, link_scale_rows, slot_hot, cell_hot)
     return seal_result, cavity_result
 
 

time: 63.1 us -> 37.6 us (0.60)
  local copies, waits for them, and re-layouts: 16 us -> 0 us
  blocking collectives: 13.5 us -> 0 us
  starting transfers between devices: 11.1 us -> 16.1 us
  Pallas kernels: 20.8 us -> 18.7 us
  waiting for transfers between devices: 0.01 us -> 1.7 us
    unnamed x46 -> x0, local copies, waits for them, and re-layouts: 15.3 us -> none
    all_to_all x1 -> x0, blocking collectives: 13.5 us -> none  [exchange(): lax.all_to_all(shaped, 'circ', split_axis=0, concat_axis=0, tiled=True)]
    all_to_all x1 -> x2, starting transfers between devices: 4.79 us -> 12 us  [exchange(): lax.all_to_all(shaped, 'circ', split_axis=0, concat_axis=0, tiled=True)]
    ppermute x2, starting transfers between devices: 6.26 us -> 4.07 us  [the longest x1 3.05 us: on_device(): outer = lax.ppermute(faces, 'axial', swaps(1))]
    pallas_call x7, Pallas kernels: 20.8 us -> 18.7 us  [the longest x1 5.05 us: on_device(): pl.pallas_call(functools.partial(seal_add_kernel, halo_rows, sectors), in...]
    all_to_all x1 -> x2, waiting for transfers between devices: 0.01 us -> 1.59 us  [exchange(): lax.all_to_all(shaped, 'circ', split_axis=0, concat_axis=0, tiled=True)]
    squeeze x1 -> x0, local copies, waits for them, and re-layouts: 0.69 us -> none  [on_device(): halo_operands = halos if halos else (seal_scales[0, :1], seal_scales[0, :1])]
  transfers between devices with their start and end apart: 3 -> 4, of which waited for: 0 -> 2; matrix products, arithmetic and copies ran while one was open for 1% -> 0% of each run, Pallas kernels for 13% -> 29%
where the time goes in v1:
time: 37.6 us; the launch traced here: 37.2 us
  Pallas kernels  18.7 us (50%)
  starting transfers between devices  16.1 us (43%)
  waiting for transfers between devices  1.7 us (5%)
  between operations  0.7 us (2%)
    all_to_all x2, starting transfers between devices, exchange(): lax.all_to_all(shaped, 'circ', split_axis=0, concat_axis=0, tiled=True)  12 us
    pallas_call x1, Pallas kernels, on_device(): pl.pallas_call(functools.partial(seal_add_kernel, halo_rows, sectors), in...  5.05 us
    pallas_call x1, Pallas kernels, on_device(): pl.pallas_call(functools.partial(interface_kernel, sectors, halo_rows), i...  3.24 us
    ppermute x1, starting transfers between devices, on_device(): outer = lax.ppermute(faces, 'axial', swaps(1))  3.05 us
    pallas_call x1, Pallas kernels, on_device(): pl.pallas_call(functools.partial(answer_kernel, width), in_specs=[VMEM] *...  2.96 us
    pallas_call x1, Pallas kernels, on_device(): pl.pallas_call(cavity_kernel, in_specs=[HBM] * 11, out_specs=[VMEM] * 7,...  2.34 us
    pallas_call x1, Pallas kernels, on_device(): pl.pallas_call(functools.partial(seal_kernel, 16), in_specs=[VMEM] * 6, o...  2.09 us
    pallas_call x1, Pallas kernels, on_device(): pl.pallas_call(functools.partial(cavity_add_kernel, 8), in_specs=[VMEM] *...  1.75 us
  transfers between devices with their start and end apart: 4, of which 2 were waited for; matrix products, arithmetic and copies ran while one was open for 0% of the time, Pallas kernels for 29%

profile of v1, /device:TPU:1, one launch (start us, length us, event | category | flops | bytes accessed | tf_op | source)
XLA Modules:
  0.0 37.2 jit_solution(15463927909067097029)
XLA Ops:
  0.6 3.2 %interface.1 = (f32[512,128]{1,0:T(8,128)}, s32[16,128]{1,0:T(8,128)S(1)}) custom-call(s32[16,128]{1,0:T(8,128)} %bitcast.17, s32[16,128]{1,0:T(8,128)} %bitcast.18, s32[16,128]{1,0:T(8,128)} %bitcast.15, f32[12,1024]{1,0:T(8,128)} %state_hbm.5, bf16[36,2,2048]{2,1,0:T(2,128)(2,1)} %bitcast.12, f32[2,2048]{1,0:T(2,128)} %link_scales_hbm.1, ...), custom_call_target="tpu_custom_call" | custom-call | tf_op jit(solution)/shard_map/interface/pallas_call | solution.py:493
  3.9 6.4 %all-to-all-start = ((f32[8,64,128]{2,1,0:T(8,128)}), f32[8,64,128]{2,1,0:T(8,128)S(1)}, u32[]{:S(2)}, u32[]{:S(2)}) async-start(f32[8,64,128]{2,1,0:T(8,128)} %bitcast.4), calls=%async_computation | async-start | bytes 524288 | tf_op jit(solution)/shard_map/all_to_all | solution.py:451
  10.2 1.3 %faces.1 = (f32[64,128]{1,0:T(8,128)S(1)}, f32[12,64,128]{2,1,0:T(8,128)S(1)}, bf16[2,384,256]{2,1,0:T(8,128)(2,1)S(1)}) custom-call(f32[12,64,128]{2,1,0:T(8,128)} %state_hbm.4), custom_call_target="tpu_custom_call" | custom-call | tf_op jit(solution)/shard_map/faces/pallas_call | solution.py:513
  11.5 1.0 %collective-permute-start = (f32[64,128]{1,0:T(8,128)S(1)}, f32[64,128]{1,0:T(8,128)S(1)}, u32[]{:S(2)}, u32[]{:S(2)}) collective-permute-start(f32[64,128]{1,0:T(8,128)S(1)} %get-tuple-element.27), channel_id=1, source_target_pairs={{0,1},{1,0},{2,3},{3,2},{4,5},{5,4},{6,7},{7,6},{8,9},{9,8},{10,11... | collective-permute-start | bytes 98312 | tf_op jit(solution)/shard_map/ppermute | solution.py:529
  12.6 3.0 %collective-permute-start.1 = (f32[64,128]{1,0:T(8,128)S(1)}, f32[64,128]{1,0:T(8,128)S(1)}, u32[]{:S(2)}, u32[]{:S(2)}) collective-permute-start(f32[64,128]{1,0:T(8,128)S(1)} %get-tuple-element.27), channel_id=1, source_target_pairs={{1,2},{2,1},{5,6},{6,5},{9,10},{10,9},{13,14},{14,13},{17,18},{18,... | collective-permute-start | bytes 98312 | tf_op jit(solution)/shard_map/ppermute | solution.py:530
  15.6 2.3 %cavity.1 = (f32[12,1024]{1,0:T(8,128)S(1)}, f32[576,128]{1,0:T(8,128)S(1)}, f32[32,128]{1,0:T(8,128)S(1)}, s32[16,128]{1,0:T(8,128)S(1)}, bf16[5,36,64,128]{3,2...) custom-call(f32[12,1024]{1,0:T(8,128)} %state_hbm.5, bf16[5,36,1024]{2,1,0:T(8,128)(2,1)} %blocks_hbm.1, ...), custom_call_target="tpu_custom_call" | custom-call | flops 1000000 | bytes 10000000 | tf_op jit(solution)/shard_map/cavity/pallas_call | solution.py:543
  18.0 0.0 collective-permute-done.inner
  18.0 0.1 collective-permute-done.1.outer
  18.1 2.1 %seal.1 = (f32[12,64,128]{2,1,0:T(8,128)S(1)}, f32[80,128]{1,0:T(8,128)S(1)}) custom-call(f32[12,64,128]{2,1,0:T(8,128)S(1)} %get-tuple-element.23.state, bf16[5,36,64,128]{3,2,1,0:T(8,128)(2,1)S(1)} %get-tuple-element.24.blocks, f32[5,64,128]{2,1,0:T(8,128)S(1)} %get-tuple-element.25.scales, f32[64,128]{1,0:T(8,128)S(1)} %get-tuple-element.26.volume, ...), custom_call_target="tpu_custom_call" | custom-call | flops 1000000 | bytes 10000000 | tf_op jit(solution)/shard_map/seal/pallas_call | solution.py:567
  20.2 0.0 all-to-all-done
  20.2 3.0 %answers.1 = f32[384,128]{1,0:T(8,128)} custom-call(bf16[2,384,256]{2,1,0:T(8,128)(2,1)S(1)} %get-tuple-element.37.table, f32[512,128]{1,0:T(8,128)S(1)} %bitcast.9), custom_call_target="tpu_custom_call" | custom-call | tf_op jit(solution)/shard_map/answers/pallas_call | solution.py:583
  23.1 5.6 %all-to-all-start.1 = ((f32[8,48,128]{2,1,0:T(8,128)}), f32[8,48,128]{2,1,0:T(8,128)S(1)}, u32[]{:S(2)}, u32[]{:S(2)}) async-start(f32[8,48,128]{2,1,0:T(8,128)} %bitcast.14), calls=%async_computation.1 | async-start | bytes 393216 | tf_op jit(solution)/shard_map/all_to_all | solution.py:451
  28.8 5.0 %seal_add.1 = (f32[12,64,128]{2,1,0:T(8,128)}, bf16[256,2048]{1,0:T(8,128)(2,1)S(1)}, bf16[256,2048]{1,0:T(8,128)(2,1)S(1)}) custom-call(f32[12,64,128]{2,1,0:T(8,128)S(1)} %get-tuple-element.30.part, f32[512,128]{1,0:T(8,128)S(1)} %bitcast.10, f32[80,128]{1,0:T(8,128)S(1)} %get-tuple-element.32.edges, s32[16,128]{1,0:T(8,128)S(1)} %get-tuple-element.33.slots, ...), custom_call_target="tpu_custom_call" | custom-call | flops 1000000 | bytes 10000000 | tf_op jit(solution)/shard_map/seal_add/pallas_call | solution.py:598
  33.8 1.6 %all-to-all-done.1 = f32[8,48,128]{2,1,0:T(8,128)S(1)} async-done(((f32[8,48,128]{2,1,0:T(8,128)}), f32[8,48,128]{2,1,0:T(8,128)S(1)}, u32[]{:S(2)}, u32[]{:S(2)}) %all-to-all-start.1) | async-done | bytes 196640 | tf_op jit(solution)/shard_map/all_to_all | solution.py:451
  35.4 1.8 %cavity_add.1 = f32[12,1024]{1,0:T(8,128)} custom-call(f32[12,1024]{1,0:T(8,128)S(1)} %get-tuple-element.36.part, f32[384,128]{1,0:T(8,128)S(1)} %bitcast.11, s32[16,128]{1,0:T(8,128)S(1)} %get-tuple-element.33.slots, s32[16,128]{1,0:T(8,128)S(1)} %get-tuple-element.34.cavity_index, f32[576,128]{1,0:T(8,128)S(1)} %get-tuple-element.38.link_rows, ...), custom_call_target="tpu_custom_call" | custom-call | tf_op jit(solution)/shard_map/cavity_add/pallas_call | solution.py:613
Async XLA Ops:
  3.9 16.3 %all-to-all-start = ((f32[8,64,128]{2,1,0:T(8,128)}), f32[8,64,128]{2,1,0:T(8,128)S(1)}, u32[]{:S(2)}, u32[]{:S(2)}) async-start(f32[8,64,128]{2,1,0:T(8,128)} %bitcast.4), calls=%async_computation | async-start | bytes 524288 | tf_op jit(solution)/shard_map/all_to_all | solution.py:451
  11.5 6.4 %collective-permute-start = (f32[64,128]{1,0:T(8,128)S(1)}, f32[64,128]{1,0:T(8,128)S(1)}, u32[]{:S(2)}, u32[]{:S(2)}) collective-permute-start(f32[64,128]{1,0:T(8,128)S(1)} %get-tuple-element.27), channel_id=1, source_target_pairs={{0,1},{1,0},{2,3},{3,2},{4,5},{5,4},{6,7},{7,6},{8,9},{9,8},{10,11... | collective-permute-start | bytes 98312 | tf_op jit(solution)/shard_map/ppermute | solution.py:529
  12.6 5.5 %collective-permute-start.1 = (f32[64,128]{1,0:T(8,128)S(1)}, f32[64,128]{1,0:T(8,128)S(1)}, u32[]{:S(2)}, u32[]{:S(2)}) collective-permute-start(f32[64,128]{1,0:T(8,128)S(1)} %get-tuple-element.27), channel_id=1, source_target_pairs={{1,2},{2,1},{5,6},{6,5},{9,10},{10,9},{13,14},{14,13},{17,18},{18,... | collective-permute-start | bytes 98312 | tf_op jit(solution)/shard_map/ppermute | solution.py:530
  23.1 12.3 %all-to-all-start.1 = ((f32[8,48,128]{2,1,0:T(8,128)}), f32[8,48,128]{2,1,0:T(8,128)S(1)}, u32[]{:S(2)}, u32[]{:S(2)}) async-start(f32[8,48,128]{2,1,0:T(8,128)} %bitcast.14), calls=%async_computation.1 | async-start | bytes 393216 | tf_op jit(solution)/shard_map/all_to_all | solution.py:451

commit v2 on v1

--- a/solution.py
+++ b/solution.py
@@ -7,7 +7,7 @@
 from jax.sharding import PartitionSpec as P
 
 whirl_rate = 0.6
-F32, BF16, I32 = jnp.float32, jnp.bfloat16, jnp.int32
+F32, BF16, I32, I16 = jnp.float32, jnp.bfloat16, jnp.int32, jnp.int16
 LANES = 128
 WIDE = 256
 PARAMS = pltpu.CompilerParams(vmem_limit_bytes=16 * 1024 * 1024)
@@ -31,6 +31,30 @@
 def halves(value):
     high = value.astype(BF16).astype(F32)
     return high, value - high
+
+
+def coded(values):
+    top = functools.reduce(jnp.maximum, [jnp.abs(v) for v in values])
+    power = jnp.ceil(jnp.log2(jnp.maximum(top, 2.0**-100) * (1.0 / 32000.0)))
+    factor = jnp.exp2(-power)
+    return [jnp.round(v * factor) for v in values], power
+
+
+def integer_halves(value):
+    high = 256.0 * jnp.floor(value * (1.0 / 256.0))
+    return high, value - high
+
+
+def narrow(value):
+    return value.astype(I32).astype(I16)
+
+
+def widen(value):
+    return value.astype(I32).astype(F32)
+
+
+def chunk_base(chunk, block):
+    return (chunk // 4) * block + (chunk % 4) * 16
 
 
 def product_into(totals, entry, factor, vector):
@@ -60,10 +84,9 @@
 
 def interface_kernel(
     sectors, halo_rows, owner_hbm, seal_index_hbm, cavity_index_hbm, state_hbm, blocks_hbm,
-    scales_hbm, seal_hbm, send, slots, block_rows, scale_rows, state_rows, left, right,
-    owner, seal_index, cavity_index, state, blocks, scales, first, last, arrivals,
+    scales_hbm, seal_hbm, send, slots, seal, block_rows, scale_rows, state_rows, left, right,
+    wide, owner, seal_index, cavity_index, state, blocks, scales, arrivals,
 ):
-    last_row = seal_hbm.shape[1]
     loads = start_loads(
         (
             (owner_hbm, owner),
@@ -72,8 +95,7 @@
             (state_hbm, state),
             (cavity_index_hbm, cavity_index),
             (seal_index_hbm, seal_index),
-            (seal_hbm.at[:, 0:8, :], first),
-            (seal_hbm.at[:, last_row - 8 : last_row, :], last),
+            (seal_hbm, seal),
         ),
         arrivals,
     )
@@ -94,7 +116,7 @@
         place = jnp.sum(hot[c] * (prefix[part] + offset), axis=0, keepdims=True)
         slots[c : c + 1, :] = owner[c : c + 1, :] * capacity + place.astype(I32)
         offset = offset + totals[part]
-    for load in loads[1:]:
+    for load in loads[1:-1]:
         load.wait()
     for entry in range(36):
         both = blocks[entry].astype(F32)
@@ -116,8 +138,9 @@
     terms = product_into(
         [None] * 12, lambda e: block_rows[e * rows : (e + 1) * rows, :], scale_rows[0:rows, :], vector
     )
-    terms.append(seal_index[...].astype(F32))
-    parts = [half for term in terms for half in halves(term)]
+    terms, power = coded(terms)
+    terms = terms + [seal_index[...].astype(F32), power]
+    parts = [half for term in terms for half in integer_halves(term)]
     groups = 2 * rows * LANES // WIDE
     for c in range(rows):
         slot = slots[c : c + 1, :]
@@ -131,21 +154,29 @@
     moved = lax.dot_general(
         left[...], right[...], (((1,), (1,)), ((), ())), preferred_element_type=F32
     )
-    for number in range(13):
+    for number in range(14):
         pair = moved[2 * number * groups : (2 * number + 2) * groups]
         value = pair[:groups] + pair[groups:]
         for half in range(2):
-            send[pl.ds(half * 16 + number, groups, stride=32), :] = value[
+            wide[pl.ds(half * 16 + number, groups, stride=32), :] = value[
                 :, half * LANES : (half + 1) * LANES
             ]
-    for number in range(13, 16):
-        send[pl.ds(number, 2 * groups, stride=16), :] = jnp.zeros((2 * groups, LANES), F32)
+    for number in range(14, 16):
+        wide[pl.ds(number, 2 * groups, stride=16), :] = jnp.zeros((2 * groups, LANES), F32)
+    loads[-1].wait()
+    block = send.shape[0] * 2 // groups
+    for at in range(0, groups // 2):
+        send[at * block : at * block + 64, :] = narrow(wide[at * 64 : at * 64 + 64, :])
     if halo_rows:
         me = lax.axis_index("circ")
-        for step, edge, row in ((1, last, 7), (sectors - 1, first, 0)):
-            base = lax.rem(me + step, sectors) * 64
-            for f in range(12):
-                send[pl.ds(base + (f // 3) * 16 + 13 + f % 3, 1), :] = edge[f, row : row + 1, :]
+        zero = jnp.zeros((16, LANES), I16)
+        for at in range(0, groups // 2):
+            send[at * block + 64 : at * block + 80, :] = zero
+        for step, row in ((1, seal.shape[1] - 1), (sectors - 1, 0)):
+            base = pl.multiple_of(lax.rem(me + step, sectors) * block + 64, 16)
+            values, power = coded([seal[f, row : row + 1, :] for f in range(12)])
+            tile = jnp.concatenate(values + [power] + [jnp.zeros((3, LANES), F32)], axis=0)
+            send[pl.ds(base, 16), :] = narrow(tile)
 
 
 def start_loads(pairs, arrivals):
@@ -158,40 +189,35 @@
     return loads
 
 
-def face_kernel(state_hbm, faces, state, table, arrivals):
-    (load,) = start_loads([(state_hbm, state)], arrivals)
-    load.wait()
+def face_kernel(state, faces, table):
     lane = iota(faces.shape, 1)
     half_rows = faces.shape[0] // 2
     total = jnp.zeros(faces.shape, F32)
     for f in range(12):
-        own = state[f]
-        total = jnp.where(lane == f, pltpu.roll(own, f + 1, 1), total)
-        total = jnp.where(lane == 16 + f, pltpu.roll(own, 16 + f, 1), total)
-        at = pl.ds(f * half_rows, half_rows)
-        for half in range(2):
-            high, low = halves(own[half * half_rows : (half + 1) * half_rows, :])
-            table[0, at, half * LANES : (half + 1) * LANES] = high.astype(BF16)
-            table[1, at, half * LANES : (half + 1) * LANES] = low.astype(BF16)
+        total = jnp.where(lane == f, pltpu.roll(state[f], f + 1, 1), total)
+        total = jnp.where(lane == 16 + f, pltpu.roll(state[f], 16 + f, 1), total)
     faces[...] = total
-
-
-def seal_kernel(step_rows, state, blocks, scales, volume, inner, outer, out, edges, beside, along):
+    for half in range(2):
+        here = slice(half * half_rows, (half + 1) * half_rows)
+        values, power = coded([state[f, here, :] for f in range(12)])
+        for f, value in enumerate(values + [power]):
+            high, low = integer_halves(value)
+            at = pl.ds(f * half_rows, half_rows)
+            table[at, half * LANES : (half + 1) * LANES] = high.astype(BF16)
+            table[at, WIDE + half * LANES : WIDE + (half + 1) * LANES] = low.astype(BF16)
+
+
+def seal_kernel(step_rows, state, blocks, scales, volume, out, edges, beside, along):
     rows = state.shape[1]
     lane = iota((rows, LANES), 1)
-    odd = lax.rem(lax.axis_index("axial"), 2) == 1
-    low = jnp.where(odd, inner[...], outer[...])
-    high = jnp.where(odd, outer[...], inner[...])
     for f in range(12):
         beside[0, f, 1:rows, :] = state[f, 0 : rows - 1, :]
         beside[0, f, 0:1, :] = jnp.zeros((1, LANES), F32)
         beside[1, f, 0 : rows - 1, :] = state[f, 1:rows, :]
         beside[1, f, rows - 1 : rows, :] = jnp.zeros((1, LANES), F32)
         own = state[f]
-        edge = pltpu.roll(low, (LANES - f) % LANES, 1)
-        along[0, f] = jnp.where(lane == 0, edge, pltpu.roll(own, 1, 1))
-        edge = pltpu.roll(high, LANES - 1 - 16 - f, 1)
-        along[1, f] = jnp.where(lane == LANES - 1, edge, pltpu.roll(own, LANES - 1, 1))
+        along[0, f] = jnp.where(lane == 0, 0.0, pltpu.roll(own, 1, 1))
+        along[1, f] = jnp.where(lane == LANES - 1, 0.0, pltpu.roll(own, LANES - 1, 1))
 
     def add_rows(step, carry):
         here = pl.ds(pl.multiple_of(step * step_rows, step_rows), step_rows)
@@ -220,35 +246,68 @@
         edges[first + 37 : first + 40, :] = jnp.zeros((3, LANES), F32)
 
 
+def end_columns_kernel(step_rows, part, blocks, scales, inner, outer, out):
+    odd = lax.rem(lax.axis_index("axial"), 2) == 1
+
+    def add_rows(step, carry):
+        here = pl.ds(pl.multiple_of(step * step_rows, step_rows), step_rows)
+        first, second = inner[here, :], outer[here, :]
+        low, high = jnp.where(odd, first, second), jnp.where(odd, second, first)
+        lane = iota((step_rows, LANES), 1)
+        left_half = lane < LANES // 2
+        vector = []
+        for f in range(12):
+            left = pltpu.roll(low, (LANES - f) % LANES, 1)
+            right = pltpu.roll(high, LANES - 1 - 16 - f, 1)
+            vector.append(jnp.where(lane == 0, left, jnp.where(lane == LANES - 1, right, 0.0)))
+        totals = product_into(
+            [part[f, here, :] for f in range(12)],
+            lambda e: jnp.where(
+                left_half, blocks[3, e, here, :].astype(F32), blocks[4, e, here, :].astype(F32)
+            ),
+            jnp.where(left_half, scales[3, here, :], scales[4, here, :]),
+            vector,
+        )
+        for f in range(12):
+            out[f, here, :] = totals[f]
+        return carry
+
+    lax.fori_loop(0, part.shape[1] // step_rows, add_rows, 0)
+
+
 def pick(table, hot, here):
-    found = jnp.dot(table[0], hot, preferred_element_type=F32)
-    found = found + jnp.dot(table[1], hot, preferred_element_type=F32)
+    found = jnp.dot(table[...], jnp.concatenate([hot, hot], axis=0), preferred_element_type=F32)
     bands = here.shape[0]
     return [
         jnp.sum(jnp.where(here, found[f * bands : (f + 1) * bands, :], 0.0), axis=0, keepdims=True)
-        for f in range(12)
+        for f in range(table.shape[0] // bands)
     ]
 
 
-def answer_kernel(width, table, arrived, send_hbm, send, sent):
-    chunks = arrived.shape[0] // 16
-    half_rows = table.shape[1] // 12
+def answer_kernel(width, block, table, arrived, send_hbm, wide, send, sent):
+    chunks = wide.shape[0] // 16
+    half_rows = table.shape[0] // 13
     copies = []
+    for number in range(13, 16):
+        wide[pl.ds(number, chunks, stride=16), :] = jnp.zeros((chunks, LANES), F32)
     for base in range(0, chunks, width):
-        cell = jnp.concatenate(
-            [arrived[g * 16 + 12 : g * 16 + 13, :] for g in range(base, base + width)], axis=1
-        ).astype(I32)
+        cell = []
+        for g in range(base, base + width):
+            at = chunk_base(g, block)
+            cell.append(arrived[at : at + 16, :].astype(I32)[12:13, :])
+        cell = jnp.concatenate(cell, axis=1)
         row = cell >> 7
         upper = row >= half_rows
         index = (cell & (LANES - 1)) + jnp.where(upper, LANES, 0)
         row = row - jnp.where(upper, half_rows, 0)
         here = iota((half_rows, width * LANES), 0) == row
         value = pick(table, one_hot(index), here)
-        for f in range(12):
+        for f in range(13):
             for part in range(width):
-                at = (base + part) * 12 + f
-                send[at : at + 1, :] = value[f][:, part * LANES : (part + 1) * LANES]
-        done = pl.ds(base * 12, width * 12)
+                at = (base + part) * 16 + f
+                wide[at : at + 1, :] = value[f][:, part * LANES : (part + 1) * LANES]
+        done = pl.ds(base * 16, width * 16)
+        send[done, :] = narrow(wide[done, :])
         copies.append(
             pltpu.make_async_copy(send.at[done, :], send_hbm.at[done, :], sent.at[base // width])
         )
@@ -258,11 +317,11 @@
 
 
 def seal_add_kernel(
-    halo_rows, sectors, part, arrived, edges, slots, cavity_index,
+    halo_rows, sectors, block, part, arrived, edges, slots, cavity_index,
     *refs,
 ):
     *halos, out, slot_hot, cell_hot, left, right, total = refs
-    chunks = arrived.shape[0] // 16
+    chunks = arrived.shape[0] // block * 4
     rows = part.shape[1]
     half_rows = rows // 2
     total[...] = jnp.zeros_like(total)
@@ -270,9 +329,11 @@
 
     def add_chunks(step, carry):
         for sub in range(deep):
-            tile = arrived[pl.ds(pl.multiple_of((step * deep + sub) * 16, 16), 16), :]
-            high, low = halves(tile)
-            cell = tile[12:13, :].astype(I32)
+            base = pl.multiple_of(step * (deep // 4 * block) + chunk_base(sub, block), 16)
+            tile = arrived[pl.ds(base, 16), :].astype(I32)
+            cell = tile[12:13, :]
+            tile = tile.astype(F32)
+            high, low = halves(tile * jnp.exp2(tile[13:14, :]))
             row = cell >> 7
             column = (cell & (LANES - 1)) + jnp.where(row >= half_rows, LANES, 0)
             row = jnp.where(row >= half_rows, row - half_rows, row)
@@ -305,10 +366,10 @@
     me = lax.axis_index("circ")
     for number, step in ((1, sectors - 1), (2, 1)):
         if halo_rows:
-            base = lax.rem(me + step, sectors) * 64
-            vector = [
-                arrived[pl.ds(base + (f // 3) * 16 + 13 + f % 3, 1), :] for f in range(12)
-            ]
+            base = pl.multiple_of(lax.rem(me + step, sectors) * block + 64, 16)
+            tile = widen(arrived[pl.ds(base, 16), :])
+            tile = tile * jnp.exp2(tile[12:13, :])
+            vector = [tile[f : f + 1, :] for f in range(12)]
         else:
             vector = [halos[number - 1][f] for f in range(12)]
         at = 0 if number == 1 else rows - 1
@@ -397,17 +458,19 @@
 
 def cavity_add_kernel(
     width, part, arrived, slots, cavity_index, link_rows, scale_rows, slot_hot, cell_hot,
-    out, left, table, found,
+    out, left, table, found, wide,
 ):
     rows = slots.shape[0]
-    chunks = arrived.shape[0] // 12
+    chunks = arrived.shape[0] // 16
     groups = chunks // 2
-    for f in range(12):
-        for half in range(2):
-            high, low = halves(arrived[pl.ds(half * 12 + f, groups, stride=24), :])
+    wide[...] = widen(arrived[...])
+    for half in range(2):
+        factor = jnp.exp2(wide[pl.ds(half * 16 + 12, groups, stride=32), :])
+        for f in range(12):
+            high, low = halves(wide[pl.ds(half * 16 + f, groups, stride=32), :] * factor)
             at = pl.ds(f * groups, groups)
-            table[0, at, half * LANES : (half + 1) * LANES] = high.astype(BF16)
-            table[1, at, half * LANES : (half + 1) * LANES] = low.astype(BF16)
+            table[at, half * LANES : (half + 1) * LANES] = high.astype(BF16)
+            table[at, WIDE + half * LANES : WIDE + (half + 1) * LANES] = low.astype(BF16)
     for base in range(0, rows, width):
         slot = jnp.concatenate([slots[c : c + 1, :] for c in range(base, base + width)], axis=1)
         here = iota((groups, width * LANES), 0) == (slot >> 8)
@@ -444,17 +507,16 @@
         out[:, cols] = part[:, cols] + (added[b * 32 : b * 32 + 12] + added[b * 32 + 16 : b * 32 + 28])
 
 
-def exchange(values, sectors, features):
-    chunks = values.shape[0] // features
+def exchange(values, sectors, chunks):
     if sectors <= chunks:
-        shaped = values.reshape(sectors, chunks // sectors * features, LANES)
+        shaped = values.reshape(sectors, -1, LANES)
         moved = lax.all_to_all(shaped, "circ", split_axis=0, concat_axis=0, tiled=True)
         return moved.reshape(values.shape)
     each = sectors // chunks
-    shaped = values.reshape(chunks, features, each, LANES // each).transpose(0, 2, 1, 3)
-    shaped = shaped.reshape(sectors, features, LANES // each)
+    shaped = values.reshape(chunks, 16, each, LANES // each).transpose(0, 2, 1, 3)
+    shaped = shaped.reshape(sectors, 16, LANES // each)
     moved = lax.all_to_all(shaped, "circ", split_axis=0, concat_axis=0, tiled=True)
-    moved = moved.reshape(chunks, each, features, LANES // each).transpose(0, 2, 1, 3)
+    moved = moved.reshape(chunks, each, 16, LANES // each).transpose(0, 2, 1, 3)
     return moved.reshape(values.shape)
 
 
@@ -490,39 +552,42 @@
 
     hbm = lambda a: pltpu.with_memory_space_constraint(a, pltpu.HBM)
     head = (owner, seal_index, cavity_index, cavity_state, pair_blocks, link_scales)
-    send, slots = pl.pallas_call(
+    block = 80 if halo_rows else 64
+    send, slots, state = pl.pallas_call(
         functools.partial(interface_kernel, sectors, halo_rows),
         in_specs=[HBM] * 7,
-        out_specs=[VMEM, VMEM],
-        out_shape=[shape((groups * 32, LANES), F32), shape((rows, LANES), I32)],
+        out_specs=[VMEM] * 3,
+        out_shape=[
+            shape((groups // 2 * block, LANES), I16),
+            shape((rows, LANES), I32),
+            shape(seal_state.shape, F32),
+        ],
         scratch_shapes=[
             pltpu.VMEM((72 * rows, LANES), F32),
             pltpu.VMEM((2 * rows, LANES), F32),
             pltpu.VMEM((12 * cells // LANES, LANES), F32),
-            pltpu.VMEM((26 * groups, count), BF16),
+            pltpu.VMEM((28 * groups, count), BF16),
             pltpu.VMEM((WIDE, count), BF16),
+            pltpu.VMEM((groups * 32, LANES), F32),
         ]
         + [pltpu.VMEM(a.shape, a.dtype) for a in head]
-        + [pltpu.VMEM((12, 8, LANES), F32)] * 2
-        + [pltpu.SemaphoreType.DMA((8,))],
+        + [pltpu.SemaphoreType.DMA((7,))],
         compiler_params=PARAMS,
         name="interface",
     )(*[hbm(a) for a in head], hbm(seal_state))
-    arrived = exchange(send, sectors, 16)
-
-    faces, state, table = pl.pallas_call(
+    arrived = exchange(send, sectors, 2 * groups)
+
+    faces, table = pl.pallas_call(
         face_kernel,
-        in_specs=[HBM],
-        out_specs=[VMEM] * 3,
+        in_specs=[VMEM],
+        out_specs=[VMEM] * 2,
         out_shape=[
             shape((seal_rows, LANES), F32),
-            shape(seal_state.shape, F32),
-            shape((2, 6 * seal_rows, WIDE), BF16),
+            shape((13 * seal_rows // 2, 2 * WIDE), BF16),
         ],
-        scratch_shapes=[pltpu.SemaphoreType.DMA((1,))],
         compiler_params=PARAMS,
         name="faces",
-    )(hbm(seal_state))
+    )(state)
     swaps = lambda begin: [
         pair for i in range(begin, segments - 1, 2) for pair in ((i, i + 1), (i + 1, i))
     ]
@@ -566,7 +631,7 @@
 
     seal_part, edges = pl.pallas_call(
         functools.partial(seal_kernel, 16),
-        in_specs=[VMEM] * 6,
+        in_specs=[VMEM] * 4,
         out_specs=[VMEM] * 2,
         out_shape=[shape(seal_state.shape, F32), shape((80, LANES), F32)],
         scratch_shapes=[
@@ -576,27 +641,36 @@
         compiler_params=PARAMS,
         cost_estimate=pl.CostEstimate(flops=10**6, bytes_accessed=10**7, transcendentals=0),
         name="seal",
-    )(state, kept_blocks, kept_scales, kept_volume, inner, outer)
+    )(state, kept_blocks, kept_scales, kept_volume)
+    seal_part = pl.pallas_call(
+        functools.partial(end_columns_kernel, 16),
+        in_specs=[VMEM] * 5,
+        out_specs=VMEM,
+        out_shape=shape(seal_state.shape, F32),
+        compiler_params=PARAMS,
+        name="end_columns",
+    )(seal_part, kept_blocks, kept_scales, inner, outer)
 
     arrived, seal_part, cavity_part = lax.optimization_barrier((arrived, seal_part, cavity_part))
     width = 8
     answers = pl.pallas_call(
-        functools.partial(answer_kernel, width),
+        functools.partial(answer_kernel, width, block),
         in_specs=[VMEM] * 2,
         out_specs=HBM,
-        out_shape=pltpu.HBM((groups * 24, LANES), F32),
+        out_shape=pltpu.HBM((groups * 32, LANES), I16),
         scratch_shapes=[
-            pltpu.VMEM((groups * 24, LANES), F32),
+            pltpu.VMEM((groups * 32, LANES), F32),
+            pltpu.VMEM((groups * 32, LANES), I16),
             pltpu.SemaphoreType.DMA((2 * groups // width,)),
         ],
         compiler_params=PARAMS,
         name="answers",
     )(table, arrived)
-    returned = exchange(answers, sectors, 12)
-
-    deep = 4
+    returned = exchange(answers, sectors, 2 * groups)
+
+    deep = 8
     seal_result, slot_hot, cell_hot = pl.pallas_call(
-        functools.partial(seal_add_kernel, halo_rows, sectors),
+        functools.partial(seal_add_kernel, halo_rows, sectors, block),
         in_specs=[VMEM] * (5 + len(halos)),
         out_specs=[VMEM] * 3,
         out_shape=[shape(seal_state.shape, F32)] + [shape((WIDE, count), BF16)] * 2,
@@ -617,8 +691,9 @@
         out_shape=shape((12, cells), F32),
         scratch_shapes=[
             pltpu.VMEM((32 * cells // WIDE, count), BF16),
-            pltpu.VMEM((2, 12 * groups, WIDE), BF16),
+            pltpu.VMEM((12 * groups, 2 * WIDE), BF16),
             pltpu.VMEM((12 * rows, LANES), F32),
+            pltpu.VMEM((groups * 32, LANES), F32),
         ],
         compiler_params=PARAMS,
         name="cavity_add",

time: 37.6 us -> 36.8 us (0.979)
  Pallas kernels: 18.7 us -> 18 us
    pallas_call x4 -> x5, Pallas kernels: 11.4 us -> 10.5 us  [the longest x1 4.66 us: on_device(): pl.pallas_call(functools.partial(seal_add_kernel, halo_rows, sectors, blo...]
  transfers between devices with their start and end apart: 4 -> 4, of which waited for: 2 -> 1; matrix products, arithmetic and copies ran while one was open for 0% -> 0% of each run, Pallas kernels for 29% -> 27%
where the time goes in v2:
time: 36.8 us; the launch traced here: 36.4 us
  Pallas kernels  18 us (49%)
  starting transfers between devices  16.2 us (44%)
  waiting for transfers between devices  1.55 us (4%)
  between operations  0.71 us (2%)
    all_to_all x2, starting transfers between devices, exchange(): lax.all_to_all(shaped, 'circ', split_axis=0, concat_axis=0, tiled=True)  12.1 us
    pallas_call x1, Pallas kernels, on_device(): pl.pallas_call(functools.partial(seal_add_kernel, halo_rows, sectors, blo...  4.66 us
    pallas_call x1, Pallas kernels, on_device(): pl.pallas_call(functools.partial(interface_kernel, sectors, halo_rows), i...  3.29 us
    pallas_call x1, Pallas kernels, on_device(): pl.pallas_call(functools.partial(answer_kernel, width, block), in_specs=[...  3.06 us
    ppermute x1, starting transfers between devices, on_device(): outer = lax.ppermute(faces, 'axial', swaps(1))  3.05 us
    pallas_call x1, Pallas kernels, on_device(): pl.pallas_call(cavity_kernel, in_specs=[HBM] * 11, out_specs=[VMEM] * 7,...  2.34 us
    pallas_call x1, Pallas kernels, on_device(): pl.pallas_call(functools.partial(seal_kernel, 16), in_specs=[VMEM] * 4, o...  1.9 us
    pallas_call x1, Pallas kernels, on_device(): pl.pallas_call(functools.partial(cavity_add_kernel, 8), in_specs=[VMEM] *...  1.87 us
  transfers between devices with their start and end apart: 4, of which 1 were waited for; matrix products, arithmetic and copies ran while one was open for 0% of the time, Pallas kernels for 27%

profile of v2, /device:TPU:1, one launch (start us, length us, event | category | flops | bytes accessed | tf_op | source)
XLA Modules:
  0.0 36.4 jit_solution(8442964416266737162)
XLA Ops:
  0.6 3.3 %interface.1 = (s16[640,128]{1,0:T(8,128)(2,1)}, s32[16,128]{1,0:T(8,128)S(1)}, f32[12,64,128]{2,1,0:T(8,128)S(1)}) custom-call(s32[16,128]{1,0:T(8,128)} %bitcast.17, s32[16,128]{1,0:T(8,128)} %bitcast.18, s32[16,128]{1,0:T(8,128)} %bitcast.15, f32[12,1024]{1,0:T(8,128)} %state_hbm.3, bf16[36,2,2048]{2,1,0:T(2,128)(2,1)} %bitcast.12, ...), custom_call_target="tpu_custom_call" | custom-call | tf_op jit(solution)/shard_map/interface/pallas_call | solution.py:556
  3.9 6.4 %all-to-all-start = ((s16[8,80,128]{2,1,0:T(8,128)(2,1)}), s16[8,80,128]{2,1,0:T(8,128)(2,1)S(1)}, u32[]{:S(2)}, u32[]{:S(2)}) async-start(s16[8,80,128]{2,1,0:T(8,128)(2,1)} %bitcast.4), calls=%async_computation | async-start | bytes 327680 | tf_op jit(solution)/shard_map/all_to_all | solution.py:513
  10.3 0.3 faces.1
  10.6 1.0 %collective-permute-start = (f32[64,128]{1,0:T(8,128)S(1)}, f32[64,128]{1,0:T(8,128)S(1)}, u32[]{:S(2)}, u32[]{:S(2)}) collective-permute-start(f32[64,128]{1,0:T(8,128)S(1)} %get-tuple-element.28), channel_id=1, source_target_pairs={{0,1},{1,0},{2,3},{3,2},{4,5},{5,4},{6,7},{7,6},{8,9},{9,8},{10,11... | collective-permute-start | bytes 98312 | tf_op jit(solution)/shard_map/ppermute | solution.py:594
  11.6 3.0 %collective-permute-start.1 = (f32[64,128]{1,0:T(8,128)S(1)}, f32[64,128]{1,0:T(8,128)S(1)}, u32[]{:S(2)}, u32[]{:S(2)}) collective-permute-start(f32[64,128]{1,0:T(8,128)S(1)} %get-tuple-element.28), channel_id=1, source_target_pairs={{1,2},{2,1},{5,6},{6,5},{9,10},{10,9},{13,14},{14,13},{17,18},{18,... | collective-permute-start | bytes 98312 | tf_op jit(solution)/shard_map/ppermute | solution.py:595
  14.7 2.3 %cavity.1 = (f32[12,1024]{1,0:T(8,128)S(1)}, f32[576,128]{1,0:T(8,128)S(1)}, f32[32,128]{1,0:T(8,128)S(1)}, s32[16,128]{1,0:T(8,128)S(1)}, bf16[5,36,64,128]{3,2...) custom-call(f32[12,1024]{1,0:T(8,128)} %state_hbm.3, bf16[5,36,1024]{2,1,0:T(8,128)(2,1)} %blocks_hbm.1, ...), custom_call_target="tpu_custom_call" | custom-call | flops 1000000 | bytes 10000000 | tf_op jit(solution)/shard_map/cavity/pallas_call | solution.py:608
  17.0 1.9 %seal.1 = (f32[12,64,128]{2,1,0:T(8,128)S(1)}, f32[80,128]{1,0:T(8,128)S(1)}) custom-call(f32[12,64,128]{2,1,0:T(8,128)S(1)} %get-tuple-element.23.state, bf16[5,36,64,128]{3,2,1,0:T(8,128)(2,1)S(1)} %get-tuple-element.24.blocks, f32[5,64,128]{2,1,0:T(8,128)S(1)} %get-tuple-element.25.scales, f32[64,128]{1,0:T(8,128)S(1)} %get-tuple-element.26.volume), custom_call_target="tpu_custom_call" | custom-call | flops 1000000 | bytes 10000000 | tf_op jit(solution)/shard_map/seal/pallas_call | solution.py:632
  19.0 0.0 collective-permute-done.inner
  19.0 0.0 collective-permute-done.1.outer
  19.0 0.5 %end_columns.1.part = f32[12,64,128]{2,1,0:T(8,128)S(1)} custom-call(f32[12,64,128]{2,1,0:T(8,128)S(1)} %get-tuple-element.27.part, bf16[5,36,64,128]{3,2,1,0:T(8,128)(2,1)S(1)} %get-tuple-element.24.blocks, f32[5,64,128]{2,1,0:T(8,128)S(1)} %get-tuple-element.25.scales, f32[64,128]{1,0:T(8,128)S(1)} %collective-permute-done.inner, ...), custom_call_target="tpu_custom_call" | custom-call | tf_op jit(solution)/shard_map/end_columns/pallas_call | solution.py:645
  19.5 0.0 all-to-all-done
  19.5 3.1 %answers.1 = s16[512,128]{1,0:T(8,128)(2,1)} custom-call(bf16[416,512]{1,0:T(8,128)(2,1)S(1)} %get-tuple-element.37.table, s16[640,128]{1,0:T(8,128)(2,1)S(1)} %bitcast.9), custom_call_target="tpu_custom_call" | custom-call | tf_op jit(solution)/shard_map/answers/pallas_call | solution.py:656
  22.6 5.7 %all-to-all-start.1 = ((s16[8,64,128]{2,1,0:T(8,128)(2,1)}), s16[8,64,128]{2,1,0:T(8,128)(2,1)S(1)}, u32[]{:S(2)}, u32[]{:S(2)}) async-start(s16[8,64,128]{2,1,0:T(8,128)(2,1)} %bitcast.14), calls=%async_computation.1 | async-start | bytes 262144 | tf_op jit(solution)/shard_map/all_to_all | solution.py:513
  28.3 4.7 %seal_add.1 = (f32[12,64,128]{2,1,0:T(8,128)}, bf16[256,2048]{1,0:T(8,128)(2,1)S(1)}, bf16[256,2048]{1,0:T(8,128)(2,1)S(1)}) custom-call(f32[12,64,128]{2,1,0:T(8,128)S(1)} %end_columns.1.part, s16[640,128]{1,0:T(8,128)(2,1)S(1)} %bitcast.10, f32[80,128]{1,0:T(8,128)S(1)} %get-tuple-element.32.edges, s32[16,128]{1,0:T(8,128)S(1)} %get-tuple-element.33.slots, ...), custom_call_target="tpu_custom_call" | custom-call | flops 1000000 | bytes 10000000 | tf_op jit(solution)/shard_map/seal_add/pallas_call | solution.py:672
  33.0 1.5 %all-to-all-done.1 = s16[8,64,128]{2,1,0:T(8,128)(2,1)S(1)} async-done(((s16[8,64,128]{2,1,0:T(8,128)(2,1)}), s16[8,64,128]{2,1,0:T(8,128)(2,1)S(1)}, u32[]{:S(2)}, u32[]{:S(2)}) %all-to-all-start.1) | async-done | bytes 131104 | tf_op jit(solution)/shard_map/all_to_all | solution.py:513
  34.5 1.9 %cavity_add.1 = f32[12,1024]{1,0:T(8,128)} custom-call(f32[12,1024]{1,0:T(8,128)S(1)} %get-tuple-element.36.part, s16[512,128]{1,0:T(8,128)(2,1)S(1)} %bitcast.11, s32[16,128]{1,0:T(8,128)S(1)} %get-tuple-element.33.slots, s32[16,128]{1,0:T(8,128)S(1)} %get-tuple-element.34.cavity_index, f32[576,128]{1,0:T(8,128)S(1)} %get-tuple-element.38.link_rows, ...), custom_call_target="tpu_custom_call" | custom-call | tf_op jit(solution)/shard_map/cavity_add/pallas_call | solution.py:687
Async XLA Ops:
  3.9 15.6 %all-to-all-start = ((s16[8,80,128]{2,1,0:T(8,128)(2,1)}), s16[8,80,128]{2,1,0:T(8,128)(2,1)S(1)}, u32[]{:S(2)}, u32[]{:S(2)}) async-start(s16[8,80,128]{2,1,0:T(8,128)(2,1)} %bitcast.4), calls=%async_computation | async-start | bytes 327680 | tf_op jit(solution)/shard_map/all_to_all | solution.py:513
  10.6 8.3 %collective-permute-start = (f32[64,128]{1,0:T(8,128)S(1)}, f32[64,128]{1,0:T(8,128)S(1)}, u32[]{:S(2)}, u32[]{:S(2)}) collective-permute-start(f32[64,128]{1,0:T(8,128)S(1)} %get-tuple-element.28), channel_id=1, source_target_pairs={{0,1},{1,0},{2,3},{3,2},{4,5},{5,4},{6,7},{7,6},{8,9},{9,8},{10,11... | collective-permute-start | bytes 98312 | tf_op jit(solution)/shard_map/ppermute | solution.py:594
  11.6 7.3 %collective-permute-start.1 = (f32[64,128]{1,0:T(8,128)S(1)}, f32[64,128]{1,0:T(8,128)S(1)}, u32[]{:S(2)}, u32[]{:S(2)}) collective-permute-start(f32[64,128]{1,0:T(8,128)S(1)} %get-tuple-element.28), channel_id=1, source_target_pairs={{1,2},{2,1},{5,6},{6,5},{9,10},{10,9},{13,14},{14,13},{17,18},{18,... | collective-permute-start | bytes 98312 | tf_op jit(solution)/shard_map/ppermute | solution.py:595
  22.6 11.9 %all-to-all-start.1 = ((s16[8,64,128]{2,1,0:T(8,128)(2,1)}), s16[8,64,128]{2,1,0:T(8,128)(2,1)S(1)}, u32[]{:S(2)}, u32[]{:S(2)}) async-start(s16[8,64,128]{2,1,0:T(8,128)(2,1)} %bitcast.14), calls=%async_computation.1 | async-start | bytes 262144 | tf_op jit(solution)/shard_map/all_to_all | solution.py:513

commit v3 on v2

--- a/solution.py
+++ b/solution.py
@@ -84,8 +84,10 @@
 
 def interface_kernel(
     sectors, halo_rows, owner_hbm, seal_index_hbm, cavity_index_hbm, state_hbm, blocks_hbm,
-    scales_hbm, seal_hbm, send, slots, seal, block_rows, scale_rows, state_rows, left, right,
-    wide, owner, seal_index, cavity_index, state, blocks, scales, arrivals,
+    scales_hbm, seal_hbm, tile_blocks_hbm, tile_scales_hbm, tile_links_hbm, tile_volume_hbm,
+    send, slots, seal, cavity_index, state, tile_blocks, tile_scales, tile_links, tile_volume,
+    block_rows, scale_rows, state_rows, left, right, wide, owner, seal_index, blocks, scales,
+    arrivals,
 ):
     loads = start_loads(
         (
@@ -96,6 +98,10 @@
             (cavity_index_hbm, cavity_index),
             (seal_index_hbm, seal_index),
             (seal_hbm, seal),
+            (tile_blocks_hbm, tile_blocks),
+            (tile_scales_hbm, tile_scales),
+            (tile_links_hbm, tile_links),
+            (tile_volume_hbm, tile_volume),
         ),
         arrivals,
     )
@@ -116,7 +122,7 @@
         place = jnp.sum(hot[c] * (prefix[part] + offset), axis=0, keepdims=True)
         slots[c : c + 1, :] = owner[c : c + 1, :] * capacity + place.astype(I32)
         offset = offset + totals[part]
-    for load in loads[1:-1]:
+    for load in loads[1:6]:
         load.wait()
     for entry in range(36):
         both = blocks[entry].astype(F32)
@@ -163,7 +169,8 @@
             ]
     for number in range(14, 16):
         wide[pl.ds(number, 2 * groups, stride=16), :] = jnp.zeros((2 * groups, LANES), F32)
-    loads[-1].wait()
+    for load in loads[6:]:
+        load.wait()
     block = send.shape[0] * 2 // groups
     for at in range(0, groups // 2):
         send[at * block : at * block + 64, :] = narrow(wide[at * 64 : at * 64 + 64, :])
@@ -318,9 +325,14 @@
 
 def seal_add_kernel(
     halo_rows, sectors, block, part, arrived, edges, slots, cavity_index,
+    link_blocks_hbm, link_scales_hbm,
     *refs,
 ):
-    *halos, out, slot_hot, cell_hot, left, right, total = refs
+    *halos, out, slot_hot, cell_hot, link_rows, link_scale_rows = refs[:-6]
+    left, right, total, link_blocks, link_scales, arrivals = refs[-6:]
+    loads = start_loads(
+        ((link_blocks_hbm, link_blocks), (link_scales_hbm, link_scales)), arrivals
+    )
     chunks = arrived.shape[0] // block * 4
     rows = part.shape[1]
     half_rows = rows // 2
@@ -363,6 +375,16 @@
         )
         out[f, 0:half_rows, :] = part[f, 0:half_rows, :] + added[:, :LANES]
         out[f, half_rows:rows, :] = part[f, half_rows:rows, :] + added[:, LANES:]
+    for load in loads:
+        load.wait()
+    row_count = link_blocks.shape[2] // LANES
+    for entry in range(36):
+        both = link_blocks[entry].astype(F32)
+        for c in range(row_count):
+            link_rows[entry * row_count + c : entry * row_count + c + 1, :] = both[
+                1:2, c * LANES : (c + 1) * LANES
+            ]
+    fold_cells(link_scales, link_scale_rows, 2, 0, row_count * LANES)
     me = lax.axis_index("circ")
     for number, step in ((1, sectors - 1), (2, 1)):
         if halo_rows:
@@ -385,30 +407,18 @@
 
 
 def cavity_kernel(
-    state_hbm, blocks_hbm, scales_hbm, links_hbm, volume_hbm, link_blocks_hbm, link_scales_hbm,
-    index_hbm, seal_blocks_hbm, seal_scales_hbm, seal_volume_hbm,
-    out, link_rows, link_scale_rows, cavity_index, seal_blocks, seal_scales, seal_volume,
-    state_rows, block_rows, scale_rows, face_rows, out_rows,
-    state, blocks, scales, links, volume, link_blocks, link_scales, arrivals,
+    state, blocks, scales, links, volume, seal_blocks_hbm, seal_scales_hbm, seal_volume_hbm,
+    out, seal_blocks, seal_scales, seal_volume,
+    state_rows, block_rows, scale_rows, face_rows, out_rows, arrivals,
 ):
     loads = start_loads(
         (
-            (state_hbm, state),
-            (links_hbm, links),
-            (blocks_hbm, blocks),
-            (scales_hbm, scales),
-            (volume_hbm, volume),
-            (link_blocks_hbm, link_blocks),
-            (link_scales_hbm, link_scales),
-            (index_hbm, cavity_index),
+            (seal_blocks_hbm, seal_blocks),
             (seal_scales_hbm, seal_scales),
             (seal_volume_hbm, seal_volume),
-            (seal_blocks_hbm, seal_blocks),
         ),
         arrivals,
     )
-    for load in loads[:7]:
-        load.wait()
     cells = state.shape[1]
     rows = cells // LANES
     fold_cells(state, state_rows, 12, 0, cells)
@@ -444,15 +454,7 @@
         out_rows[f * rows : (f + 1) * rows, :] = totals[f]
     for c in range(rows):
         out[:, c * LANES : (c + 1) * LANES] = out_rows[pl.ds(c, 12, stride=rows), :]
-    row_count = link_blocks.shape[2] // LANES
-    for entry in range(36):
-        both = link_blocks[entry].astype(F32)
-        for c in range(row_count):
-            link_rows[entry * row_count + c : entry * row_count + c + 1, :] = both[
-                1:2, c * LANES : (c + 1) * LANES
-            ]
-    fold_cells(link_scales, link_scale_rows, 2, 0, row_count * LANES)
-    for load in loads[7:]:
+    for load in loads:
         load.wait()
 
 
@@ -553,15 +555,17 @@
     hbm = lambda a: pltpu.with_memory_space_constraint(a, pltpu.HBM)
     head = (owner, seal_index, cavity_index, cavity_state, pair_blocks, link_scales)
     block = 80 if halo_rows else 64
-    send, slots, state = pl.pallas_call(
+    preload = (cavity_blocks, cavity_scales, cavity_links, cavity_volume.reshape(-1, LANES))
+    send, slots, state, kept_index, *tile = pl.pallas_call(
         functools.partial(interface_kernel, sectors, halo_rows),
-        in_specs=[HBM] * 7,
-        out_specs=[VMEM] * 3,
+        in_specs=[HBM] * 11,
+        out_specs=[VMEM] * 9,
         out_shape=[
             shape((groups // 2 * block, LANES), I16),
             shape((rows, LANES), I32),
             shape(seal_state.shape, F32),
-        ],
+        ]
+        + [shape(a.shape, a.dtype) for a in head[2:4] + preload],
         scratch_shapes=[
             pltpu.VMEM((72 * rows, LANES), F32),
             pltpu.VMEM((2 * rows, LANES), F32),
@@ -570,11 +574,11 @@
             pltpu.VMEM((WIDE, count), BF16),
             pltpu.VMEM((groups * 32, LANES), F32),
         ]
-        + [pltpu.VMEM(a.shape, a.dtype) for a in head]
-        + [pltpu.SemaphoreType.DMA((7,))],
+        + [pltpu.VMEM(a.shape, a.dtype) for a in head[:2] + head[4:]]
+        + [pltpu.SemaphoreType.DMA((11,))],
         compiler_params=PARAMS,
         name="interface",
-    )(*[hbm(a) for a in head], hbm(seal_state))
+    )(*[hbm(a) for a in head], hbm(seal_state), *[hbm(a) for a in preload])
     arrived = exchange(send, sectors, 2 * groups)
 
     faces, table = pl.pallas_call(
@@ -602,32 +606,24 @@
             lax.ppermute(first, "circ", [((i + 1) % sectors, i) for i in range(sectors)]),
         )
 
-    tile = (cavity_state, cavity_blocks, cavity_scales, cavity_links, cavity_volume.reshape(-1, LANES))
-    tile = tile + (pair_blocks, link_scales)
-    kept = (cavity_index, seal_blocks, seal_scales, seal_volume)
-    cavity_part, link_rows, link_scale_rows, kept_index, kept_blocks, kept_scales, kept_volume = pl.pallas_call(
+    kept = (seal_blocks, seal_scales, seal_volume)
+    cavity_part, kept_blocks, kept_scales, kept_volume = pl.pallas_call(
         cavity_kernel,
-        in_specs=[HBM] * 11,
-        out_specs=[VMEM] * 7,
-        out_shape=[
-            shape((12, cells), F32),
-            shape((36 * rows, LANES), F32),
-            shape((2 * rows, LANES), F32),
-        ]
-        + [shape(a.shape, a.dtype) for a in kept],
+        in_specs=[VMEM] * 5 + [HBM] * 3,
+        out_specs=[VMEM] * 4,
+        out_shape=[shape((12, cells), F32)] + [shape(a.shape, a.dtype) for a in kept],
         scratch_shapes=[
             pltpu.VMEM((12 * cells // LANES, LANES), F32),
             pltpu.VMEM((180 * cells // LANES, LANES), F32),
             pltpu.VMEM((5 * cells // LANES, LANES), F32),
             pltpu.VMEM((4 * cells // LANES, LANES), I32),
             pltpu.VMEM((12 * cells // LANES, LANES), F32),
-        ]
-        + [pltpu.VMEM(a.shape, a.dtype) for a in tile]
-        + [pltpu.SemaphoreType.DMA((11,))],
+            pltpu.SemaphoreType.DMA((3,)),
+        ],
         compiler_params=PARAMS,
         cost_estimate=pl.CostEstimate(flops=10**6, bytes_accessed=10**7, transcendentals=0),
         name="cavity",
-    )(*[hbm(a) for a in tile + kept])
+    )(*tile, *[hbm(a) for a in kept])
 
     seal_part, edges = pl.pallas_call(
         functools.partial(seal_kernel, 16),
@@ -669,20 +665,25 @@
     returned = exchange(answers, sectors, 2 * groups)
 
     deep = 8
-    seal_result, slot_hot, cell_hot = pl.pallas_call(
+    seal_result, slot_hot, cell_hot, link_rows, link_scale_rows = pl.pallas_call(
         functools.partial(seal_add_kernel, halo_rows, sectors, block),
-        in_specs=[VMEM] * (5 + len(halos)),
-        out_specs=[VMEM] * 3,
-        out_shape=[shape(seal_state.shape, F32)] + [shape((WIDE, count), BF16)] * 2,
+        in_specs=[VMEM] * 5 + [HBM] * 2 + [VMEM] * len(halos),
+        out_specs=[VMEM] * 5,
+        out_shape=[shape(seal_state.shape, F32)]
+        + [shape((WIDE, count), BF16)] * 2
+        + [shape((36 * rows, LANES), F32), shape((2 * rows, LANES), F32)],
         scratch_shapes=[
             pltpu.VMEM((12 * seal_rows, deep * LANES), BF16),
             pltpu.VMEM((WIDE, deep * LANES), BF16),
             pltpu.VMEM((12 * seal_rows, WIDE), F32),
+            pltpu.VMEM(pair_blocks.shape, BF16),
+            pltpu.VMEM(link_scales.shape, F32),
+            pltpu.SemaphoreType.DMA((2,)),
         ],
         compiler_params=PARAMS,
         cost_estimate=pl.CostEstimate(flops=10**6, bytes_accessed=10**7, transcendentals=0),
         name="seal_add",
-    )(seal_part, arrived, edges, slots, kept_index, *halos)
+    )(seal_part, arrived, edges, slots, kept_index, hbm(pair_blocks), hbm(link_scales), *halos)
 
     cavity_result = pl.pallas_call(
         functools.partial(cavity_add_kernel, 8),

time: 36.8 us -> 36.4 us (0.989)
    pallas_call x1, Pallas kernels: 2.34 us -> 1.89 us  [on_device(): pl.pallas_call(cavity_kernel, in_specs=[VMEM] * 5 + [HBM] * 3, out_specs=...]
  transfers between devices with their start and end apart: 4 -> 4, of which waited for: 1 -> 1; matrix products, arithmetic and copies ran while one was open for 0% -> 0% of each run, Pallas kernels for 27% -> 26%
where the time goes in v3:
time: 36.4 us; the launch traced here: 36 us
  Pallas kernels  17.8 us (49%)
  starting transfers between devices  16.2 us (45%)
  waiting for transfers between devices  1.35 us (4%)
  between operations  0.72 us (2%)
    all_to_all x2, starting transfers between devices, exchange(): lax.all_to_all(shaped, 'circ', split_axis=0, concat_axis=0, tiled=True)  12.1 us
    pallas_call x1, Pallas kernels, on_device(): pl.pallas_call(functools.partial(seal_add_kernel, halo_rows, sectors, blo...  4.84 us
    pallas_call x1, Pallas kernels, on_device(): pl.pallas_call(functools.partial(interface_kernel, sectors, halo_rows), i...  3.33 us
    pallas_call x1, Pallas kernels, on_device(): pl.pallas_call(functools.partial(answer_kernel, width, block), in_specs=[...  3.05 us
    ppermute x1, starting transfers between devices, on_device(): outer = lax.ppermute(faces, 'axial', swaps(1))  3.05 us
    pallas_call x1, Pallas kernels, on_device(): pl.pallas_call(functools.partial(seal_kernel, 16), in_specs=[VMEM] * 4, o...  1.93 us
    pallas_call x1, Pallas kernels, on_device(): pl.pallas_call(cavity_kernel, in_specs=[VMEM] * 5 + [HBM] * 3, out_specs=...  1.89 us
    pallas_call x1, Pallas kernels, on_device(): pl.pallas_call(functools.partial(cavity_add_kernel, 8), in_specs=[VMEM] *...  1.85 us
  transfers between devices with their start and end apart: 4, of which 1 were waited for; matrix products, arithmetic and copies ran while one was open for 0% of the time, Pallas kernels for 26%

profile of v3, /device:TPU:1, one launch (start us, length us, event | category | flops | bytes accessed | tf_op | source)
XLA Modules:
  0.0 36.0 jit_solution(14803758632415575078)
XLA Ops:
  0.6 3.3 %interface.1 = (s16[640,128]{1,0:T(8,128)(2,1)}, s32[16,128]{1,0:T(8,128)S(1)}, f32[12,64,128]{2,1,0:T(8,128)S(1)}, s32[16,128]{1,0:T(8,128)S(1)}, f32[12,1024]{...) custom-call(s32[16,128]{1,0:T(8,128)} %bitcast.15, ...), custom_call_target="tpu_custom_call" | custom-call | tf_op jit(solution)/shard_map/interface/pallas_call | solution.py:559
  4.0 6.4 %all-to-all-start = ((s16[8,80,128]{2,1,0:T(8,128)(2,1)}), s16[8,80,128]{2,1,0:T(8,128)(2,1)S(1)}, u32[]{:S(2)}, u32[]{:S(2)}) async-start(s16[8,80,128]{2,1,0:T(8,128)(2,1)} %bitcast.5), calls=%async_computation | async-start | bytes 327680 | tf_op jit(solution)/shard_map/all_to_all | solution.py:515
  10.3 0.3 faces.1
  10.7 1.0 %collective-permute-start = (f32[64,128]{1,0:T(8,128)S(1)}, f32[64,128]{1,0:T(8,128)S(1)}, u32[]{:S(2)}, u32[]{:S(2)}) collective-permute-start(f32[64,128]{1,0:T(8,128)S(1)} %get-tuple-element.38), channel_id=1, source_target_pairs={{0,1},{1,0},{2,3},{3,2},{4,5},{5,4},{6,7},{7,6},{8,9},{9,8},{10,11... | collective-permute-start | bytes 98312 | tf_op jit(solution)/shard_map/ppermute | solution.py:598
  11.7 3.1 %collective-permute-start.1 = (f32[64,128]{1,0:T(8,128)S(1)}, f32[64,128]{1,0:T(8,128)S(1)}, u32[]{:S(2)}, u32[]{:S(2)}) collective-permute-start(f32[64,128]{1,0:T(8,128)S(1)} %get-tuple-element.38), channel_id=1, source_target_pairs={{1,2},{2,1},{5,6},{6,5},{9,10},{10,9},{13,14},{14,13},{17,18},{18,... | collective-permute-start | bytes 98312 | tf_op jit(solution)/shard_map/ppermute | solution.py:599
  14.7 1.9 %cavity.1 = (f32[12,1024]{1,0:T(8,128)S(1)}, bf16[5,36,64,128]{3,2,1,0:T(8,128)(2,1)S(1)}, f32[5,64,128]{2,1,0:T(8,128)S(1)}, f32[64,128]{1,0:T(8,128)S(1)}) custom-call(f32[12,1024]{1,0:T(8,128)S(1)} %get-tuple-element.29.state, bf16[5,36,1024]{2,1,0:T(8,128)(2,1)S(1)} %get-tuple-element.30.blocks, f32[5,1024]{1,0:T(8,128)S(1)} %get-tuple-element.31.scales, ...), custom_call_target="tpu_custom_call" | custom-call | flops 1000000 | bytes 10000000 | tf_op jit(solution)/shard_map/cavity/pallas_call | solution.py:610
  16.6 1.9 %seal.1 = (f32[12,64,128]{2,1,0:T(8,128)S(1)}, f32[80,128]{1,0:T(8,128)S(1)}) custom-call(f32[12,64,128]{2,1,0:T(8,128)S(1)} %get-tuple-element.28.state, bf16[5,36,64,128]{3,2,1,0:T(8,128)(2,1)S(1)} %get-tuple-element.34.blocks, f32[5,64,128]{2,1,0:T(8,128)S(1)} %get-tuple-element.35.scales, f32[64,128]{1,0:T(8,128)S(1)} %get-tuple-element.36.volume), custom_call_target="tpu_custom_call" | custom-call | flops 1000000 | bytes 10000000 | tf_op jit(solution)/shard_map/seal/pallas_call | solution.py:628
  18.6 0.0 collective-permute-done.inner
  18.6 0.0 collective-permute-done.1.outer
  18.6 0.5 %end_columns.1.part = f32[12,64,128]{2,1,0:T(8,128)S(1)} custom-call(f32[12,64,128]{2,1,0:T(8,128)S(1)} %get-tuple-element.37.part, bf16[5,36,64,128]{3,2,1,0:T(8,128)(2,1)S(1)} %get-tuple-element.34.blocks, f32[5,64,128]{2,1,0:T(8,128)S(1)} %get-tuple-element.35.scales, f32[64,128]{1,0:T(8,128)S(1)} %collective-permute-done.inner, ...), custom_call_target="tpu_custom_call" | custom-call | tf_op jit(solution)/shard_map/end_columns/pallas_call | solution.py:641
  19.2 0.0 all-to-all-done
  19.2 3.1 %answers.1 = s16[512,128]{1,0:T(8,128)(2,1)} custom-call(bf16[416,512]{1,0:T(8,128)(2,1)S(1)} %get-tuple-element.47.table, s16[640,128]{1,0:T(8,128)(2,1)S(1)} %bitcast.9), custom_call_target="tpu_custom_call" | custom-call | tf_op jit(solution)/shard_map/answers/pallas_call | solution.py:652
  22.2 5.7 %all-to-all-start.1 = ((s16[8,64,128]{2,1,0:T(8,128)(2,1)}), s16[8,64,128]{2,1,0:T(8,128)(2,1)S(1)}, u32[]{:S(2)}, u32[]{:S(2)}) async-start(s16[8,64,128]{2,1,0:T(8,128)(2,1)} %bitcast.14), calls=%async_computation.1 | async-start | bytes 262144 | tf_op jit(solution)/shard_map/all_to_all | solution.py:515
  28.0 4.8 %seal_add.1 = (f32[12,64,128]{2,1,0:T(8,128)}, bf16[256,2048]{1,0:T(8,128)(2,1)S(1)}, bf16[256,2048]{1,0:T(8,128)(2,1)S(1)}, f32[576,128]{1,0:T(8,128)S(1)}, f32[32,128]{1,0:T(8,128)S(1)}) custom-call(f32[12,64,128]{2,1,0:T(8,128)S(1)} %end_columns.1.part, s16[640,128]{1,0:T(8,128)(2,1)S(1)} %bitcast.10, f32[80,128]{1,0:T(8,128)S(1)} %get-tuple-element.42.edges, ...), custom_call_target="tpu_custom_call" | custom-call | flops 1000000 | bytes 10000000 | tf_op jit(solution)/shard_map/seal_add/pallas_call | solution.py:668
  32.8 1.3 %all-to-all-done.1 = s16[8,64,128]{2,1,0:T(8,128)(2,1)S(1)} async-done(((s16[8,64,128]{2,1,0:T(8,128)(2,1)}), s16[8,64,128]{2,1,0:T(8,128)(2,1)S(1)}, u32[]{:S(2)}, u32[]{:S(2)}) %all-to-all-start.1) | async-done | bytes 131104 | tf_op jit(solution)/shard_map/all_to_all | solution.py:515
  34.2 1.9 %cavity_add.1 = f32[12,1024]{1,0:T(8,128)} custom-call(f32[12,1024]{1,0:T(8,128)S(1)} %get-tuple-element.46.part, s16[512,128]{1,0:T(8,128)(2,1)S(1)} %bitcast.11, s32[16,128]{1,0:T(8,128)S(1)} %get-tuple-element.43.slots, s32[16,128]{1,0:T(8,128)S(1)} %get-tuple-element.44.cavity_index, f32[576,128]{1,0:T(8,128)S(1)} %get-tuple-element.48.link_rows, ...), custom_call_target="tpu_custom_call" | custom-call | tf_op jit(solution)/shard_map/cavity_add/pallas_call | solution.py:688
Async XLA Ops:
  4.0 15.2 %all-to-all-start = ((s16[8,80,128]{2,1,0:T(8,128)(2,1)}), s16[8,80,128]{2,1,0:T(8,128)(2,1)S(1)}, u32[]{:S(2)}, u32[]{:S(2)}) async-start(s16[8,80,128]{2,1,0:T(8,128)(2,1)} %bitcast.5), calls=%async_computation | async-start | bytes 327680 | tf_op jit(solution)/shard_map/all_to_all | solution.py:515
  10.7 7.9 %collective-permute-start = (f32[64,128]{1,0:T(8,128)S(1)}, f32[64,128]{1,0:T(8,128)S(1)}, u32[]{:S(2)}, u32[]{:S(2)}) collective-permute-start(f32[64,128]{1,0:T(8,128)S(1)} %get-tuple-element.38), channel_id=1, source_target_pairs={{0,1},{1,0},{2,3},{3,2},{4,5},{5,4},{6,7},{7,6},{8,9},{9,8},{10,11... | collective-permute-start | bytes 98312 | tf_op jit(solution)/shard_map/ppermute | solution.py:598
  11.7 6.9 %collective-permute-start.1 = (f32[64,128]{1,0:T(8,128)S(1)}, f32[64,128]{1,0:T(8,128)S(1)}, u32[]{:S(2)}, u32[]{:S(2)}) collective-permute-start(f32[64,128]{1,0:T(8,128)S(1)} %get-tuple-element.38), channel_id=1, source_target_pairs={{1,2},{2,1},{5,6},{6,5},{9,10},{10,9},{13,14},{14,13},{17,18},{18,... | collective-permute-start | bytes 98312 | tf_op jit(solution)/shard_map/ppermute | solution.py:599
  22.2 11.9 %all-to-all-start.1 = ((s16[8,64,128]{2,1,0:T(8,128)(2,1)}), s16[8,64,128]{2,1,0:T(8,128)(2,1)S(1)}, u32[]{:S(2)}, u32[]{:S(2)}) async-start(s16[8,64,128]{2,1,0:T(8,128)(2,1)} %bitcast.14), calls=%async_computation.1 | async-start | bytes 262144 | tf_op jit(solution)/shard_map/all_to_all | solution.py:515

commit v4 on v3

--- a/solution.py
+++ b/solution.py
@@ -127,8 +127,8 @@
     for entry in range(36):
         both = blocks[entry].astype(F32)
         for c in range(rows):
-            block_rows[pl.ds(entry * rows + c, 2, stride=36 * rows), :] = both[
-                :, c * LANES : (c + 1) * LANES
+            block_rows[entry * rows + c : entry * rows + c + 1, :] = both[
+                0:1, c * LANES : (c + 1) * LANES
             ]
     fold_cells(scales, scale_rows, 2, 0, rows * LANES)
     fold_cells(state, state_rows, 12, 0, state.shape[1])
@@ -567,9 +567,9 @@
         ]
         + [shape(a.shape, a.dtype) for a in head[2:4] + preload],
         scratch_shapes=[
-            pltpu.VMEM((72 * rows, LANES), F32),
-            pltpu.VMEM((2 * rows, LANES), F32),
-            pltpu.VMEM((12 * cells // LANES, LANES), F32),
+            pltpu.VMEM((36 * rows, LANES), F32),
+            pltpu.VMEM((8 * rows, LANES), F32),
+            pltpu.VMEM((16 * cells // LANES, LANES), F32),
             pltpu.VMEM((28 * groups, count), BF16),
             pltpu.VMEM((WIDE, count), BF16),
             pltpu.VMEM((groups * 32, LANES), F32),
@@ -613,11 +613,11 @@
         out_specs=[VMEM] * 4,
         out_shape=[shape((12, cells), F32)] + [shape(a.shape, a.dtype) for a in kept],
         scratch_shapes=[
-            pltpu.VMEM((12 * cells // LANES, LANES), F32),
-            pltpu.VMEM((180 * cells // LANES, LANES), F32),
-            pltpu.VMEM((5 * cells // LANES, LANES), F32),
-            pltpu.VMEM((4 * cells // LANES, LANES), I32),
-            pltpu.VMEM((12 * cells // LANES, LANES), F32),
+            pltpu.VMEM((16 * cells // LANES, LANES), F32),
+            pltpu.VMEM((184 * cells // LANES, LANES), F32),
+            pltpu.VMEM((8 * cells // LANES, LANES), F32),
+            pltpu.VMEM((8 * cells // LANES, LANES), I32),
+            pltpu.VMEM((16 * cells // LANES, LANES), F32),
             pltpu.SemaphoreType.DMA((3,)),
         ],
         compiler_params=PARAMS,
@@ -671,7 +671,7 @@
         out_specs=[VMEM] * 5,
         out_shape=[shape(seal_state.shape, F32)]
         + [shape((WIDE, count), BF16)] * 2
-        + [shape((36 * rows, LANES), F32), shape((2 * rows, LANES), F32)],
+        + [shape((36 * rows, LANES), F32), shape((8 * rows, LANES), F32)],
         scratch_shapes=[
             pltpu.VMEM((12 * seal_rows, deep * LANES), BF16),
             pltpu.VMEM((WIDE, deep * LANES), BF16),

time: 36.4 us -> 36.4 us (level)
  no operation moved by 1% of the time
where the time goes in v4:
time: 36.4 us; the launch traced here: 36 us
  Pallas kernels  17.8 us (49%)
  starting transfers between devices  16.2 us (45%)
  waiting for transfers between devices  1.35 us (4%)
  between operations  0.72 us (2%)
    all_to_all x2, starting transfers between devices, exchange(): lax.all_to_all(shaped, 'circ', split_axis=0, concat_axis=0, tiled=True)  12.1 us
    pallas_call x1, Pallas kernels, on_device(): pl.pallas_call(functools.partial(seal_add_kernel, halo_rows, sectors, blo...  4.84 us
    pallas_call x1, Pallas kernels, on_device(): pl.pallas_call(functools.partial(interface_kernel, sectors, halo_rows), i...  3.34 us
    pallas_call x1, Pallas kernels, on_device(): pl.pallas_call(functools.partial(answer_kernel, width, block), in_specs=[...  3.05 us
    ppermute x1, starting transfers between devices, on_device(): outer = lax.ppermute(faces, 'axial', swaps(1))  3.05 us
    pallas_call x1, Pallas kernels, on_device(): pl.pallas_call(functools.partial(seal_kernel, 16), in_specs=[VMEM] * 4, o...  1.93 us
    pallas_call x1, Pallas kernels, on_device(): pl.pallas_call(cavity_kernel, in_specs=[VMEM] * 5 + [HBM] * 3, out_specs=...  1.89 us
    pallas_call x1, Pallas kernels, on_device(): pl.pallas_call(functools.partial(cavity_add_kernel, 8), in_specs=[VMEM] *...  1.85 us
  transfers between devices with their start and end apart: 4, of which 1 were waited for; matrix products, arithmetic and copies ran while one was open for 0% of the time, Pallas kernels for 26%

profile of v4, /device:TPU:1, one launch (start us, length us, event | category | flops | bytes accessed | tf_op | source)
XLA Modules:
  0.0 36.0 jit_solution(1841963109947761572)
XLA Ops:
  0.6 3.3 %interface.1 = (s16[640,128]{1,0:T(8,128)(2,1)}, s32[16,128]{1,0:T(8,128)S(1)}, f32[12,64,128]{2,1,0:T(8,128)S(1)}, s32[16,128]{1,0:T(8,128)S(1)}, f32[12,1024]{...) custom-call(s32[16,128]{1,0:T(8,128)} %bitcast.15, ...), custom_call_target="tpu_custom_call" | custom-call | tf_op jit(solution)/shard_map/interface/pallas_call | solution.py:559
  4.0 6.4 %all-to-all-start = ((s16[8,80,128]{2,1,0:T(8,128)(2,1)}), s16[8,80,128]{2,1,0:T(8,128)(2,1)S(1)}, u32[]{:S(2)}, u32[]{:S(2)}) async-start(s16[8,80,128]{2,1,0:T(8,128)(2,1)} %bitcast.5), calls=%async_computation | async-start | bytes 327680 | tf_op jit(solution)/shard_map/all_to_all | solution.py:515
  10.3 0.3 faces.1
  10.7 1.0 %collective-permute-start = (f32[64,128]{1,0:T(8,128)S(1)}, f32[64,128]{1,0:T(8,128)S(1)}, u32[]{:S(2)}, u32[]{:S(2)}) collective-permute-start(f32[64,128]{1,0:T(8,128)S(1)} %get-tuple-element.38), channel_id=1, source_target_pairs={{0,1},{1,0},{2,3},{3,2},{4,5},{5,4},{6,7},{7,6},{8,9},{9,8},{10,11... | collective-permute-start | bytes 98312 | tf_op jit(solution)/shard_map/ppermute | solution.py:598
  11.7 3.0 %collective-permute-start.1 = (f32[64,128]{1,0:T(8,128)S(1)}, f32[64,128]{1,0:T(8,128)S(1)}, u32[]{:S(2)}, u32[]{:S(2)}) collective-permute-start(f32[64,128]{1,0:T(8,128)S(1)} %get-tuple-element.38), channel_id=1, source_target_pairs={{1,2},{2,1},{5,6},{6,5},{9,10},{10,9},{13,14},{14,13},{17,18},{18,... | collective-permute-start | bytes 98312 | tf_op jit(solution)/shard_map/ppermute | solution.py:599
  14.7 1.9 %cavity.1 = (f32[12,1024]{1,0:T(8,128)S(1)}, bf16[5,36,64,128]{3,2,1,0:T(8,128)(2,1)S(1)}, f32[5,64,128]{2,1,0:T(8,128)S(1)}, f32[64,128]{1,0:T(8,128)S(1)}) custom-call(f32[12,1024]{1,0:T(8,128)S(1)} %get-tuple-element.29.state, bf16[5,36,1024]{2,1,0:T(8,128)(2,1)S(1)} %get-tuple-element.30.blocks, f32[5,1024]{1,0:T(8,128)S(1)} %get-tuple-element.31.scales, ...), custom_call_target="tpu_custom_call" | custom-call | flops 1000000 | bytes 10000000 | tf_op jit(solution)/shard_map/cavity/pallas_call | solution.py:610
  16.6 1.9 %seal.1 = (f32[12,64,128]{2,1,0:T(8,128)S(1)}, f32[80,128]{1,0:T(8,128)S(1)}) custom-call(f32[12,64,128]{2,1,0:T(8,128)S(1)} %get-tuple-element.28.state, bf16[5,36,64,128]{3,2,1,0:T(8,128)(2,1)S(1)} %get-tuple-element.34.blocks, f32[5,64,128]{2,1,0:T(8,128)S(1)} %get-tuple-element.35.scales, f32[64,128]{1,0:T(8,128)S(1)} %get-tuple-element.36.volume), custom_call_target="tpu_custom_call" | custom-call | flops 1000000 | bytes 10000000 | tf_op jit(solution)/shard_map/seal/pallas_call | solution.py:628
  18.6 0.0 collective-permute-done.inner
  18.6 0.0 collective-permute-done.1.outer
  18.6 0.5 %end_columns.1.part = f32[12,64,128]{2,1,0:T(8,128)S(1)} custom-call(f32[12,64,128]{2,1,0:T(8,128)S(1)} %get-tuple-element.37.part, bf16[5,36,64,128]{3,2,1,0:T(8,128)(2,1)S(1)} %get-tuple-element.34.blocks, f32[5,64,128]{2,1,0:T(8,128)S(1)} %get-tuple-element.35.scales, f32[64,128]{1,0:T(8,128)S(1)} %collective-permute-done.inner, ...), custom_call_target="tpu_custom_call" | custom-call | tf_op jit(solution)/shard_map/end_columns/pallas_call | solution.py:641
  19.2 0.0 all-to-all-done
  19.2 3.1 %answers.1 = s16[512,128]{1,0:T(8,128)(2,1)} custom-call(bf16[416,512]{1,0:T(8,128)(2,1)S(1)} %get-tuple-element.47.table, s16[640,128]{1,0:T(8,128)(2,1)S(1)} %bitcast.9), custom_call_target="tpu_custom_call" | custom-call | tf_op jit(solution)/shard_map/answers/pallas_call | solution.py:652
  22.2 5.7 %all-to-all-start.1 = ((s16[8,64,128]{2,1,0:T(8,128)(2,1)}), s16[8,64,128]{2,1,0:T(8,128)(2,1)S(1)}, u32[]{:S(2)}, u32[]{:S(2)}) async-start(s16[8,64,128]{2,1,0:T(8,128)(2,1)} %bitcast.14), calls=%async_computation.1 | async-start | bytes 262144 | tf_op jit(solution)/shard_map/all_to_all | solution.py:515
  28.0 4.8 %seal_add.1 = (f32[12,64,128]{2,1,0:T(8,128)}, bf16[256,2048]{1,0:T(8,128)(2,1)S(1)}, bf16[256,2048]{1,0:T(8,128)(2,1)S(1)}, f32[576,128]{1,0:T(8,128)S(1)}, f32[128,128]{1,0:T(8,128)S(1)}) custom-call(f32[12,64,128]{2,1,0:T(8,128)S(1)} %end_columns.1.part, s16[640,128]{1,0:T(8,128)(2,1)S(1)} %bitcast.10, f32[80,128]{1,0:T(8,128)S(1)} %get-tuple-element.42.edges, ...), custom_call_target="tpu_custom_call" | custom-call | flops 1000000 | bytes 10000000 | tf_op jit(solution)/shard_map/seal_add/pallas_call | solution.py:668
  32.8 1.3 %all-to-all-done.1 = s16[8,64,128]{2,1,0:T(8,128)(2,1)S(1)} async-done(((s16[8,64,128]{2,1,0:T(8,128)(2,1)}), s16[8,64,128]{2,1,0:T(8,128)(2,1)S(1)}, u32[]{:S(2)}, u32[]{:S(2)}) %all-to-all-start.1) | async-done | bytes 131104 | tf_op jit(solution)/shard_map/all_to_all | solution.py:515
  34.2 1.9 %cavity_add.1 = f32[12,1024]{1,0:T(8,128)} custom-call(f32[12,1024]{1,0:T(8,128)S(1)} %get-tuple-element.46.part, s16[512,128]{1,0:T(8,128)(2,1)S(1)} %bitcast.11, s32[16,128]{1,0:T(8,128)S(1)} %get-tuple-element.43.slots, s32[16,128]{1,0:T(8,128)S(1)} %get-tuple-element.44.cavity_index, f32[576,128]{1,0:T(8,128)S(1)} %get-tuple-element.48.link_rows, ...), custom_call_target="tpu_custom_call" | custom-call | tf_op jit(solution)/shard_map/cavity_add/pallas_call | solution.py:688
Async XLA Ops:
  4.0 15.2 %all-to-all-start = ((s16[8,80,128]{2,1,0:T(8,128)(2,1)}), s16[8,80,128]{2,1,0:T(8,128)(2,1)S(1)}, u32[]{:S(2)}, u32[]{:S(2)}) async-start(s16[8,80,128]{2,1,0:T(8,128)(2,1)} %bitcast.5), calls=%async_computation | async-start | bytes 327680 | tf_op jit(solution)/shard_map/all_to_all | solution.py:515
  10.7 7.9 %collective-permute-start = (f32[64,128]{1,0:T(8,128)S(1)}, f32[64,128]{1,0:T(8,128)S(1)}, u32[]{:S(2)}, u32[]{:S(2)}) collective-permute-start(f32[64,128]{1,0:T(8,128)S(1)} %get-tuple-element.38), channel_id=1, source_target_pairs={{0,1},{1,0},{2,3},{3,2},{4,5},{5,4},{6,7},{7,6},{8,9},{9,8},{10,11... | collective-permute-start | bytes 98312 | tf_op jit(solution)/shard_map/ppermute | solution.py:598
  11.7 6.9 %collective-permute-start.1 = (f32[64,128]{1,0:T(8,128)S(1)}, f32[64,128]{1,0:T(8,128)S(1)}, u32[]{:S(2)}, u32[]{:S(2)}) collective-permute-start(f32[64,128]{1,0:T(8,128)S(1)} %get-tuple-element.38), channel_id=1, source_target_pairs={{1,2},{2,1},{5,6},{6,5},{9,10},{10,9},{13,14},{14,13},{17,18},{18,... | collective-permute-start | bytes 98312 | tf_op jit(solution)/shard_map/ppermute | solution.py:599
  22.2 11.9 %all-to-all-start.1 = ((s16[8,64,128]{2,1,0:T(8,128)(2,1)}), s16[8,64,128]{2,1,0:T(8,128)(2,1)S(1)}, u32[]{:S(2)}, u32[]{:S(2)}) async-start(s16[8,64,128]{2,1,0:T(8,128)(2,1)} %bitcast.14), calls=%async_computation.1 | async-start | bytes 262144 | tf_op jit(solution)/shard_map/all_to_all | solution.py:515
